TPU v7x, 128 devices: a whole 4x4x4 slice. The times are simulated.
128 devices in a mesh: gy: 4 (over z_hi, core), gz: 32 (over x, z_lo, y).
Axes of the slice: x: 4, y: 4, z: 4 (z_hi: 2, z_lo: 2; z = z_hi * 2 + z_lo), core: 2. Of those that a mesh axis runs over, the one named last changes fastest.
Arguments:
- velocity_hat: float32 [3, 2, 256, 256, 128], P(None, None, 'gy', 'gz'), may hold values from -3 to 3
- inflow: float32 [3], replicated, may hold values from -0.4 to 1.2, as said below
- viscosity: float32 [128, 256, 512], P('gz', 'gy'), may hold values from 0.03 to 0.3
- cot_hat: float32 [3, 2, 256, 256, 128], P(None, None, 'gy', 'gz'), may hold values from -6 to 6
- mode_mask: int32 [256, 256, 128], P('gy', 'gz'), may hold values from 0 to 1, as said below
- hub_cells: int32 [100, 3], replicated, may hold values from 0 to 511, as said below
- yaw_sector: int32 [100], replicated, may hold values from 0 to 12
- thrust: float32 [100], replicated, may hold values from 0.5 to 2
Outputs:
- adjoint_hat: float32 [3, 2, 256, 256, 128], P(None, None, 'gy', 'gz')
- thrust_grad: float32 [100], replicated
Inputs may be any that keep to these rules, and one draw needn't show every extreme that they name: `mode_mask`: 1 exactly at the modes with kx < cx, |my| < cy and |mz| < cz, where the cutoffs are drawn anew between a quarter and a third of 512, 256 and 128; 0 elsewhere. `hub_cells`: row t holds the x, y and z cells of turbine t's hub; every disk of radius 4 in the y-z plane lies inside the grid, and no two disks share a cell. `inflow`: x component within 0.8 to 1.2, y within -0.4 to 0.4, z within -0.2 to 0.2.
All inputs are finite; a program needn't handle non-finite values.
Results may differ from a plain program's by a relative error of at most 0.00013.
Values sent between devices are 32-bit elements; how exact they have to be, the bound alone decides.
A program may use at most 128 MiB of HBM per device.

v0:
```python
import math

import jax
import jax.numpy as jnp
from jax import lax
from jax.sharding import PartitionSpec as P

RADIUS = 4


SECTION_STEP = 0.24
PRECISE = lax.Precision.HIGHEST


def signed_modes(index, length):
    return jnp.where(index < length // 2, index, index - length)


def complex_table(length):
    grid = jnp.arange(length, dtype=jnp.int32)
    phase = grid[:, None] * grid[None, :] % length
    angle = 2.0 * math.pi / length * phase.astype(jnp.float32)
    cosine = jnp.cos(angle)
    sine = jnp.sin(angle)
    return jnp.stack(
        [jnp.stack([cosine, sine], axis=1), jnp.stack([-sine, cosine], axis=1)], axis=0
    )


def real_table(width_x, groups_x, length_x, scale):
    blocks = (
        jnp.arange(groups_x, dtype=jnp.int32)[:, None] * width_x
        + jnp.arange(width_x, dtype=jnp.int32)[None, :]
    )
    cells_x = jnp.arange(length_x, dtype=jnp.int32)
    phase = blocks[:, :, None] * cells_x[None, None, :] % length_x
    angle = 2.0 * math.pi / length_x * phase.astype(jnp.float32)
    weight = jnp.where(blocks == 0, 1.0, 2.0).astype(jnp.float32)[:, :, None] * scale
    table = jnp.stack([weight * jnp.cos(angle), -weight * jnp.sin(angle)], axis=1)
    return table.reshape(groups_x * 2 * width_x, length_x)


def curl_modes(spectrum, waves):
    wave_x = waves[0][:, None, None]
    wave_y = waves[1][:, None]
    wave_z = waves[2]

    def rotate(values):
        return jnp.stack(
            [
                wave_y * values[..., 2, :, :, :] - wave_z * values[..., 1, :, :, :],
                wave_z * values[..., 0, :, :, :] - wave_x * values[..., 2, :, :, :],
                wave_x * values[..., 1, :, :, :] - wave_y * values[..., 0, :, :, :],
            ],
            axis=-4,
        )

    real_part = spectrum[..., 0, :, :, :]
    imag_part = spectrum[..., 1, :, :, :]
    return jnp.stack([-rotate(imag_part), rotate(real_part)], axis=-4)


def project_modes(spectrum, waves):
    wave_x = waves[0][:, None, None]
    wave_y = waves[1][:, None]
    wave_z = waves[2]
    square = wave_x * wave_x + wave_y * wave_y + wave_z * wave_z
    inverse = (square > 0).astype(jnp.float32) / (square + (square == 0).astype(jnp.float32))
    along = (wave_x * spectrum[0] + wave_y * spectrum[1] + wave_z * spectrum[2]) * inverse
    return jnp.stack(
        [spectrum[0] - wave_x * along, spectrum[1] - wave_y * along, spectrum[2] - wave_z * along]
    )


def cross(first, second):
    return jnp.stack(
        [
            first[1] * second[2] - first[2] * second[1],
            first[2] * second[0] - first[0] * second[2],
            first[0] * second[1] - first[1] * second[0],
        ]
    )


def disk_area():
    return float(
        sum(
            (
                1
                for offset_a in range(-RADIUS, RADIUS + 1)
                for offset_b in range(-RADIUS, RADIUS + 1)
                if offset_a * offset_a + offset_b * offset_b <= RADIUS * RADIUS
            )
        )
    )


def turbine_frames(hub_cells, yaw_sector, first_z, first_y, slab_z, slab_y, length_x):
    angle = (yaw_sector.astype(jnp.float32) - 6.0) * (math.pi / 36.0)
    normal = jnp.stack([jnp.cos(angle), jnp.sin(angle), jnp.zeros_like(angle)], axis=1)
    along_x = (jnp.arange(length_x, dtype=jnp.int32)[None, :] == hub_cells[:, 0:1]).astype(
        jnp.float32
    )
    offset_z = (
        first_z
        + jnp.arange(slab_z, dtype=jnp.int32)[None, :, None]
        - hub_cells[:, 2][:, None, None]
    )
    offset_y = (
        first_y
        + jnp.arange(slab_y, dtype=jnp.int32)[None, None, :]
        - hub_cells[:, 1][:, None, None]
    )
    disk = (offset_z * offset_z + offset_y * offset_y <= RADIUS * RADIUS).astype(jnp.float32)
    return (normal, along_x, disk.reshape(disk.shape[0], slab_z * slab_y))


def disk_project(field, normal, along_x, disk):
    flat = field.reshape(3, disk.shape[1], field.shape[-1])
    columns = jnp.einsum("cpx,tx->ctp", flat, along_x, precision=PRECISE)
    return jnp.einsum("ctp,tp,tc->t", columns, disk, normal, precision=PRECISE)


def spread(weights, normal, along_x, disk, shape):
    mixed = weights[:, None, None] * normal[:, :, None] * disk[:, None, :]
    return jnp.einsum("tcp,tx->cpx", mixed, along_x, precision=PRECISE).reshape(shape)


def z_inverse(spectrum, table_z):
    moved = jnp.einsum("frabq,rqsz->fzbsa", spectrum, table_z, precision=PRECISE)
    return moved.reshape(moved.shape[0], moved.shape[1], moved.shape[2], 2 * moved.shape[4])


def y_inverse(columns, table_y):
    halves = columns.reshape(
        columns.shape[0], columns.shape[1], columns.shape[2], 2, columns.shape[3] // 2
    )
    moved = jnp.einsum("fzbra,rbsy->fzysa", halves, table_y, precision=PRECISE)
    return moved.reshape(columns.shape[0], columns.shape[1], table_y.shape[3], columns.shape[3])


def x_inverse(rows, table_x):
    return jnp.einsum("fzyk,kx->fzyx", rows, table_x, precision=PRECISE)


def x_forward(field, table_x):
    return jnp.einsum("fzyx,kx->fzyk", field, table_x, precision=PRECISE)


def y_forward(columns, table_y):
    halves = columns.reshape(
        columns.shape[0], columns.shape[1], columns.shape[2], 2, columns.shape[3] // 2
    )
    moved = jnp.einsum("fzysa,rbsy->fzbra", halves, table_y, precision=PRECISE)
    return moved.reshape(columns.shape)


def z_forward(pencils, table_z):
    halves = pencils.reshape(
        pencils.shape[0], pencils.shape[1], pencils.shape[2], 2, pencils.shape[3] // 2
    )
    return jnp.einsum("fzbsa,rqsz->frabq", halves, table_z, precision=PRECISE)


def finish_rows(columns, table_x):
    return x_inverse(
        lax.all_to_all(columns, "gy", split_axis=2, concat_axis=3, tiled=True), table_x=table_x
    )


def to_physical(groups, waves, tables):
    table_z, table_y, table_x = tables
    number = groups.shape[0]
    spectrum = jnp.concatenate([groups, curl_modes(groups, waves)], axis=1)
    spectrum = spectrum.reshape((number * 6,) + groups.shape[2:])
    columns = y_inverse(
        lax.all_to_all(z_inverse(spectrum, table_z), "gz", split_axis=1, concat_axis=2, tiled=True),
        table_y=table_y,
    )
    physical = finish_rows(columns, table_x)
    return physical.reshape((number, 6) + physical.shape[1:])


def local(velocity_hat, inflow, viscosity, cot_hat, mode_mask, hub_cells, yaw_sector, thrust):
    width_x = velocity_hat.shape[2]
    rows_y = velocity_hat.shape[3]
    cells_z = velocity_hat.shape[4]
    slab_z, slab_y, length_x = viscosity.shape
    length_y = rows_y * lax.axis_size("gz")
    index_x = lax.axis_index("gy") * width_x + jnp.arange(width_x, dtype=jnp.int32)
    index_y = lax.axis_index("gz") * rows_y + jnp.arange(rows_y, dtype=jnp.int32)
    wave_x = 2.0 * math.pi / length_x * index_x.astype(jnp.float32)
    wave_y = 2.0 * math.pi / length_y * signed_modes(index_y, length_y).astype(jnp.float32)
    wave_z = (
        2.0
        * math.pi
        / cells_z
        * signed_modes(jnp.arange(cells_z, dtype=jnp.int32), cells_z).astype(jnp.float32)
    )
    waves = (wave_x, wave_y, wave_z)
    scale = 1.0 / math.sqrt(length_x * length_y * cells_z)
    table_z = complex_table(cells_z)
    table_y = complex_table(length_y)
    table_x = real_table(width_x, lax.axis_size("gy"), length_x, scale)
    tables = (table_z, table_y, table_x)
    weight_x = jnp.where(index_x == 0, 1.0, 2.0).astype(jnp.float32)[:, None, None]
    adjoint_modes = mode_mask.astype(jnp.float32) * project_modes(cot_hat, waves)
    scaled_modes = adjoint_modes / weight_x
    flow_fields = to_physical(velocity_hat[None], waves, tables)[0]
    adjoint_fields = to_physical(scaled_modes[None], waves, tables)[0]
    velocity = flow_fields[:3] + inflow[:, None, None, None]
    vorticity = flow_fields[3:]
    pull_field = adjoint_fields[:3]
    stress_bar = -adjoint_fields[3:]
    normal, along_x, disk = turbine_frames(
        hub_cells,
        yaw_sector,
        lax.axis_index("gz") * slab_z,
        lax.axis_index("gy") * slab_y,
        slab_z,
        slab_y,
        length_x,
    )
    disk_cells = disk_area()
    speed_total, push_total = lax.psum(
        (
            disk_project(velocity, normal, along_x, disk),
            disk_project(pull_field, normal, along_x, disk),
        ),
        ("gy", "gz"),
    )
    disk_speed = speed_total / disk_cells
    thrust_grad = -0.5 * SECTION_STEP * disk_speed * jnp.abs(disk_speed) * push_total
    velocity_bar = cross(vorticity, pull_field) + spread(
        -thrust * jnp.abs(disk_speed) * push_total / disk_cells,
        normal,
        along_x,
        disk,
        velocity.shape,
    )
    vorticity_bar = cross(pull_field, velocity) + viscosity[None] * stress_bar
    columns = y_forward(
        lax.all_to_all(
            x_forward(jnp.concatenate([velocity_bar, vorticity_bar], axis=0), table_x),
            "gy",
            split_axis=3,
            concat_axis=2,
            tiled=True,
        ),
        table_y=table_y,
    )
    spectra = z_forward(
        lax.all_to_all(columns, "gz", split_axis=2, concat_axis=1, tiled=True), table_z=table_z
    )
    gradient = spectra[:3] + curl_modes(spectra[3:], waves)
    return (adjoint_modes + SECTION_STEP * gradient, thrust_grad)


def solution(mesh):
    placed = (
        P(None, None, "gy", "gz", None),
        P(),
        P("gz", "gy", None),
        P(None, None, "gy", "gz", None),
        P("gy", "gz", None),
        P(),
        P(),
        P(),
    )
    return jax.shard_map(
        local,
        mesh=mesh,
        in_specs=placed,
        out_specs=(P(None, None, "gy", "gz", None), P()),
        check_vma=False,
    )
```

profile of v0, /device:TPU:0, one launch (start us, length us, event | category | flops | bytes accessed | tf_op | source)
XLA Modules:
  0.0 483.3 jit_solution(8959551527805180894)
XLA Ops:
  16.2 8.9 %all-to-all-start = ((f32[6,128,8,128]{3,2,0,1:T(8,128)}), f32[6,128,8,128]{3,2,0,1:T(8,128)}, u32[]{:S(2)}, u32[]{:S(2)}) async-start(f32[6,128,8,128]{3,2,0,1:T(8,128)} %copy.78), calls=%async_computation | async-start | bytes 6291456 | tf_op jit(solution)/shard_map/all_to_all | solution.py:177
  31.7 36.8 %all-to-all-done = f32[6,128,8,128]{3,2,0,1:T(8,128)} async-done(((f32[6,128,8,128]{3,2,0,1:T(8,128)}), f32[6,128,8,128]{3,2,0,1:T(8,128)}, u32[]{:S(2)}, u32[]{:S(2)}) %all-to-all-start) | async-done | bytes 3145760 | tf_op jit(solution)/shard_map/all_to_all | solution.py:177
  68.5 16.8 %all-to-all-start.2 = ((f32[6,128,8,128]{3,2,0,1:T(8,128)}), f32[6,128,8,128]{3,2,0,1:T(8,128)S(1)}, u32[]{:S(2)}, u32[]{:S(2)}) async-start(f32[6,128,8,128]{3,2,0,1:T(8,128)} %copy.91), calls=%async_computation.2 | async-start | bytes 6291456 | tf_op jit(solution)/shard_map/all_to_all | solution.py:177
  92.3 7.1 %reshape.940 = f32[6,4,256,2,64]{4,3,2,1,0:T(2,128)} reshape(f32[6,4,32,8,128]{4,3,2,1,0:T(8,128)} %copy.80) | data formatting | bytes 6291456 | tf_op jit(solution)/shard_map/reshape | solution.py:135
  99.4 9.5 %copy.81 = f32[6,4,256,2,64]{2,4,3,1,0:T(8,128)} copy(f32[6,4,256,2,64]{4,3,2,1,0:T(2,128)} %reshape.940) | data formatting | bytes 6291456 | tf_op jit(solution)/shard_map/reshape | solution.py:135
  108.9 7.6 %fusion.26 = f32[6,4,256,2,64]{2,4,1,0,3:T(8,128)S(1)} fusion(f32[6,4,256,2,64]{2,4,3,1,0:T(8,128)} %copy.81, f32[1,256,2,256]{3,1,0,2:T(8,128)} %get-tuple-element.50, f32[1,256,2,256]{3,1,0,2:T(8,128)} %get-tuple-element.49), kind=kOutput, calls=%fused_computation.29 | convolution fusion | flops 4832100352 | bytes 7340032 | tf_op jit(solution)/shard_map/fzbra,rbsy->fzysa/dot_general | solution.py:138
  140.6 7.1 %reshape.945 = f32[6,4,256,2,64]{4,3,2,1,0:T(2,128)} reshape(f32[6,4,32,8,128]{4,3,2,1,0:T(8,128)} %copy.93) | data formatting | bytes 6291456 | tf_op jit(solution)/shard_map/reshape | solution.py:135
  147.7 9.5 %copy.94 = f32[6,4,256,2,64]{2,4,3,1,0:T(8,128)} copy(f32[6,4,256,2,64]{4,3,2,1,0:T(2,128)} %reshape.945) | data formatting | bytes 6291456 | tf_op jit(solution)/shard_map/reshape | solution.py:135
  157.1 7.6 %fusion.29 = f32[6,4,256,2,64]{2,4,1,0,3:T(8,128)S(1)} fusion(f32[6,4,256,2,64]{2,4,3,1,0:T(8,128)} %copy.94, f32[1,256,2,256]{3,1,0,2:T(8,128)} %get-tuple-element.50, f32[1,256,2,256]{3,1,0,2:T(8,128)} %get-tuple-element.49), kind=kOutput, calls=%fused_computation.30 | convolution fusion | flops 4832100352 | bytes 7340032 | tf_op jit(solution)/shard_map/fzbra,rbsy->fzysa/dot_general | solution.py:138
  187.6 6.8 %fusion.5 = f32[6,4,64,512]{3,2,1,0:T(8,128)} fusion(f32[512,512,1,1]{1,0,3,2:T(8,128)S(1)} %bitcast.247, f32[6,4,4,8,8,128]{5,4,3,2,1,0:T(8,128)S(1)} %bitcast.251), kind=kOutput, calls=%fused_computation.5 | convolution fusion | flops 4831838208 | bytes 7340032 | tf_op jit(solution)/shard_map/fzyk,kx->fzyx/dot_general | solution.py:143
  194.4 22.9 %all-to-all-done.3 = f32[6,4,256,128]{3,1,0,2:T(4,128)} async-done(((f32[6,4,256,128]{3,1,0,2:T(4,128)}), f32[6,4,256,128]{3,1,0,2:T(4,128)}, u32[]{:S(2)}, u32[]{:S(2)}) %all-to-all-start.3) | async-done | bytes 3145760 | tf_op jit(solution)/shard_map/all_to_all | solution.py:167
  219.9 5.4 %fusion.2 = f32[6,4,64,512]{3,2,1,0:T(8,128)S(1)} fusion(f32[512,512,1,1]{1,0,3,2:T(8,128)S(1)} %bitcast.248, f32[6,4,4,8,8,128]{5,4,3,2,1,0:T(8,128)S(1)} %bitcast.252), kind=kOutput, calls=%fused_computation.2 | convolution fusion | flops 4831838208 | bytes 7340032 | tf_op jit(solution)/shard_map/fzyk,kx->fzyx/dot_general | solution.py:143
  232.8 64.9 %all-reduce = (f32[100]{0:T(128)}, f32[100]{0:T(128)}) all-reduce(f32[100]{0:T(128)} %get-tuple-element.9, f32[100]{0:T(128)} %get-tuple-element.8), channel_id=1, replica_groups=mesh['gy'=4,'gz'=32] {'gy','gz'}, use_global_device_ids=true, to_apply=%region_1.2 | all-reduce | flops 200 | bytes 1600 | tf_op jit(solution)/shard_map/psum | solution.py:225
  303.1 6.9 %fusion.13 = f32[6,4,64,512]{3,2,1,0:T(8,128)} fusion(f32[512,512,1,1]{1,0,3,2:T(8,128)S(1)} %bitcast.249, f32[3,4,64,512]{3,2,1,0:T(8,128)S(1)} %get-tuple-element.27, f32[3,4,64,512]{3,2,1,0:T(8,128)S(1)} %maximum_add_fusion), kind=kOutput, calls=%fused_computation.15 | convolution fusion | flops 4832624640 | bytes 7340032 | tf_op jit(solution)/shard_map/fzyx,kx->fzyk/dot_general | solution.py:147
  309.9 6.8 %copy.100 = f32[6,4,64,512]{2,1,0,3:T(4,128)} copy(f32[6,4,64,512]{3,2,1,0:T(8,128)} %fusion.13) | data formatting | bytes 6291456 | tf_op jit(solution)/shard_map/fzyx,kx->fzyk/dot_general | solution.py:147
  316.7 8.5 %reshape.981 = f32[4,1,196608]{2,1,0:T(1,128)} reshape(f32[512,6,4,64]{3,2,1,0:T(4,128)} %bitcast.245) | data formatting | bytes 6291456
  325.1 42.3 %all_to_all.96 = f32[4,1,196608]{2,1,0:T(1,128)S(1)} all-to-all(f32[4,1,196608]{2,1,0:T(1,128)} %reshape.981), channel_id=1, replica_groups=mesh['gy'=4,'gz'=32] {'gy'}, dimensions={0} | all-to-all | bytes 6291456 | tf_op jit(solution)/shard_map/all_to_all | solution.py:243
  368.0 10.6 %reduce.4 = f32[4,196608]{1,0:T(4,128)} reduce(f32[4,1,196608]{2,1,0:T(1,128)S(1)} %all_to_all.96, f32[]{:T(128)} %broadcast.855), dimensions={1}, to_apply=%all_to_all.84.reduce_sub_computation | reduce | bytes 6291460 | tf_op jit(solution)/shard_map/all_to_all | solution.py:243
  378.6 8.9 %reshape.982 = f32[512,6,4,64]{3,2,1,0:T(4,128)} reshape(f32[4,196608]{1,0:T(4,128)} %reduce.4) | data formatting | bytes 6291456
  387.5 5.1 %copy.101 = f32[6,4,64,4,128]{4,2,3,1,0:T(8,128)S(1)} copy(f32[6,4,64,4,128]{2,1,0,4,3:T(4,128)} %bitcast.246) | data formatting | bytes 6291456 | tf_op jit(solution)/shard_map/all_to_all | solution.py:243
  397.7 8.2 %copy.103 = f32[6,4,256,2,64]{2,4,3,1,0:T(8,128)S(1)} copy(f32[6,4,256,2,64]{4,3,2,1,0:T(2,128)} %reshape.950) | data formatting | bytes 6291456 | tf_op jit(solution)/shard_map/reshape | solution.py:151
  405.9 6.5 %fusion.32 = f32[6,4,256,2,64]{2,4,1,0,3:T(8,128)S(1)} fusion(f32[6,4,256,2,64]{2,4,3,1,0:T(8,128)S(1)} %copy.103, f32[1,256,2,256]{3,1,0,2:T(8,128)} %get-tuple-element.50, f32[1,256,2,256]{3,1,0,2:T(8,128)} %get-tuple-element.49), kind=kOutput, calls=%fused_computation.31 | convolution fusion | flops 4832100352 | bytes 7340032 | tf_op jit(solution)/shard_map/fzysa,rbsy->fzbra/dot_general | solution.py:154
  415.7 43.1 %all_to_all.97 = f32[6,4,256,128]{3,1,0,2:T(4,128)S(1)} all-to-all(f32[6,4,256,128]{3,1,0,2:T(4,128)} %copy.105), channel_id=1, replica_groups=mesh['gy'=4,'gz'=32] {'gz'}, dimensions={2} | all-to-all | bytes 6291456 | tf_op jit(solution)/shard_map/all_to_all | solution.py:253
  464.9 14.1 %fusion.36 = f32[6,2,64,8,128]{4,2,3,1,0:T(8,128)S(1)} fusion(f32[6,128,8,2,64,1]{4,3,2,1,0,5:T(2,128)} %bitcast.244, f32[1,128,2,128]{3,1,0,2:T(8,128)} %copy-done.11, f32[1,128,2,128]{3,1,0,2:T(8,128)S(1)} %get-tuple-element.51), kind=kOutput, calls=%fused_computation.33 | convolution fusion | flops 2415984640 | bytes 6553600 | tf_op jit(solution)/shard_map/fzbsa,rqsz->frabq/dot_general | solution.py:162
  (132 shorter events, 110.0 us)
Async XLA Ops:
  3.3 1.0 copy-start.14
  3.9 0.9 copy-start.9
  4.3 0.8 copy-start.5
  4.3 1.0 copy-start.7
  4.4 1.7 copy-start.4
  6.7 1.1 copy-start.13
  7.9 18.3 %copy-start.11 = (f32[1,128,2,128]{3,1,0,2:T(8,128)}, f32[1,128,2,128]{3,1,0,2:T(8,128)S(1)}, u32[]{:S(2)}) copy-start(f32[1,128,2,128]{3,1,0,2:T(8,128)S(1)} %get-tuple-element.52) | copy-start | bytes 393220
  16.2 52.3 %all-to-all-start = ((f32[6,128,8,128]{3,2,0,1:T(8,128)}), f32[6,128,8,128]{3,2,0,1:T(8,128)}, u32[]{:S(2)}, u32[]{:S(2)}) async-start(f32[6,128,8,128]{3,2,0,1:T(8,128)} %copy.78), calls=%async_computation | async-start | bytes 6291456 | tf_op jit(solution)/shard_map/all_to_all | solution.py:177
  68.5 59.2 %all-to-all-start.2 = ((f32[6,128,8,128]{3,2,0,1:T(8,128)}), f32[6,128,8,128]{3,2,0,1:T(8,128)S(1)}, u32[]{:S(2)}, u32[]{:S(2)}) async-start(f32[6,128,8,128]{3,2,0,1:T(8,128)} %copy.91), calls=%async_computation.2 | async-start | bytes 6291456 | tf_op jit(solution)/shard_map/all_to_all | solution.py:177
  127.7 1.6 copy-start.2
  129.3 43.2 %all-to-all-start.1 = ((f32[6,4,256,128]{3,1,0,2:T(4,128)}), f32[6,4,256,128]{3,1,0,2:T(4,128)S(1)}, u32[]{:S(2)}, u32[]{:S(2)}) async-start(f32[6,4,256,128]{3,1,0,2:T(4,128)} %copy.83), calls=%async_computation.1 | async-start | bytes 6291456 | tf_op jit(solution)/shard_map/all_to_all | solution.py:167
  172.5 1.7 copy-start
  174.2 43.1 %all-to-all-start.3 = ((f32[6,4,256,128]{3,1,0,2:T(4,128)}), f32[6,4,256,128]{3,1,0,2:T(4,128)}, u32[]{:S(2)}, u32[]{:S(2)}) async-start(f32[6,4,256,128]{3,1,0,2:T(4,128)} %copy.96), calls=%async_computation.3 | async-start | bytes 6291456 | tf_op jit(solution)/shard_map/all_to_all | solution.py:167
  181.8 0.8 copy-start.17
  182.5 0.6 copy-start.18
  184.5 2.4 copy-start.1
  219.8 5.4 %copy-start.3 = (f32[6,4,64,512]{3,2,1,0:T(8,128)S(1)}, f32[6,4,64,512]{3,2,1,0:T(8,128)}, u32[]{:S(2)}) copy-start(f32[6,4,64,512]{3,2,1,0:T(8,128)} %fusion.5) | copy-start | bytes 9437188
  225.2 1.5 copy-start.20
  227.0 1.0 copy-start.12
  228.9 2.0 copy-start.16
  228.9 3.3 copy-start.15
  479.0 1.0 copy-start.6
  479.0 1.2 copy-start.8
  479.0 1.3 copy-start.10
  (1 other events, 0.6 us)
where the time goes:
time: 488 us; the launch traced here: 483 us
  blocking collectives  150 us (31%)
  local copies, waits for them, and re-layouts  133 us (27%)
  matrix products  65.8 us (13%)
  waiting for transfers between devices  64.6 us (13%)
  starting transfers between devices  35.4 us (7%)
  other arithmetic  32.7 us (7%)
    psum x1, blocking collectives, local(): lax.psum((disk_project(velocity, normal, along_x, disk), disk_project(pul...  64.9 us
    all_to_all x1, blocking collectives, local(): lax.all_to_all(columns, 'gz', split_axis=2, concat_axis=1, tiled=True)  43.1 us
    all_to_all x1, blocking collectives, local(): lax.all_to_all(x_forward(jnp.concatenate([velocity_bar, vorticity_bar], a...  42.3 us
    all_to_all x2, waiting for transfers between devices, to_physical(): lax.all_to_all(z_inverse(spectrum, table_z), 'gz', split_axis=1, concat_a...  41 us
    reshape x4, local copies, waits for them, and re-layouts, y_inverse(): columns.reshape(columns.shape[0], columns.shape[1], columns.shape[2], 2,...  33.1 us
    unnamed x47, local copies, waits for them, and re-layouts  27 us
    all_to_all x2, starting transfers between devices, to_physical(): lax.all_to_all(z_inverse(spectrum, table_z), 'gz', split_axis=1, concat_a...  25.7 us
    all_to_all x2, waiting for transfers between devices, finish_rows(): lax.all_to_all(columns, 'gy', split_axis=2, concat_axis=3, tiled=True)  23.6 us
  transfers between devices with their start and end apart: 4, of which 4 were waited for; matrix products, arithmetic and copies ran while one was open for 20% of the time, Pallas kernels for 0%

commit v1 on v0

v1 whole, which is shorter than its diff:
```python
import math

import jax
import jax.numpy as jnp
import ml_dtypes
import numpy as np
from jax import lax
from jax.experimental import pallas as pl
from jax.experimental.pallas import tpu as pltpu
from jax.sharding import PartitionSpec as P

MESH = pl.DeviceIdType.MESH
F32 = jnp.float32
BF16 = jnp.bfloat16
RADIUS = 4
SECTION_STEP = 0.24
NX, NY, NZ = 512, 256, 128
WIDTH = 64
RING, RINGS = 8, 16


def disk_area():
    reach = range(-RADIUS, RADIUS + 1)
    return float(sum(1 for a in reach for b in reach if a * a + b * b <= RADIUS * RADIUS))


def signed(index, length):
    return np.where(index < length // 2, index, index - length)


def split(table):
    high = table.astype(ml_dtypes.bfloat16)
    low = (table - high.astype(np.float64)).astype(ml_dtypes.bfloat16)
    return np.stack([high, low])


def tables():
    e, w = np.meshgrid(np.arange(RING), np.arange(RINGS), indexing="ij")
    cell_z = ((w // 4) * 32 + (e // 4) * 16 + (w % 4) * 4 + e % 4).reshape(-1)
    mode_z = np.arange(NZ)
    wave_z = 2.0 * math.pi / NZ * signed(mode_z, NZ)
    angle = 2.0 * math.pi / NZ * (cell_z[:, None] * mode_z[None, :] % NZ)
    cos, sin = np.cos(angle), np.sin(angle)
    z_inverse = np.block([[cos, sin], [-wave_z * sin, wave_z * cos]])
    cos, sin = cos.T, sin.T
    wave_z = wave_z[:, None]
    z_first = np.block([cos, -sin, -wave_z * sin, -wave_z * cos])
    z_second = np.block([cos, -sin, wave_z * sin, wave_z * cos])
    row = np.arange(NY)
    w, z_lo, r = row // 16, row // 8 % 2, row % 8
    mode_y = (w // 4) * 64 + z_lo * 32 + (w % 4) * 8 + r
    angle = 2.0 * math.pi / NY * (np.arange(NY)[:, None] * mode_y[None, :] % NY)
    cos, sin = np.cos(angle), np.sin(angle)
    y_inverse = np.concatenate([cos, sin])
    y_forward = np.concatenate([cos.T, sin.T])
    lane = np.arange(NX)
    mode_x = lane // 128 * WIDTH + lane % WIDTH
    weight = np.where(mode_x == 0, 1.0, 2.0) / math.sqrt(NX * NY * NZ)
    angle = 2.0 * math.pi / NX * (mode_x[:, None] * np.arange(NX)[None, :] % NX)
    real = (lane % 128 < WIDTH)[:, None]
    x_inverse = weight[:, None] * np.where(real, np.cos(angle), -np.sin(angle))
    return [split(t) for t in (z_inverse, np.stack([z_first, z_second]), y_inverse, y_forward, x_inverse, x_inverse.T)]


def halves(value):
    high = value.astype(BF16)
    return high, (value - high.astype(F32)).astype(BF16)


def dot(left, right):
    return jnp.dot(left, right, preferred_element_type=F32)


def dot_nt(left, right):
    return lax.dot_general(left, right, (((1,), (1,)), ((), ())), preferred_element_type=F32)


def three(left, right, product=dot):
    return product(left[0], right[0]) + product(left[0], right[1]) + product(left[1], right[0])


def kernel(
    modes_ref, inflow_ref, visc_ref, cot_ref, mask_ref, turb_ref,
    zi_ref, zf_ref, yi_ref, yf_ref, xi_ref, xf_ref,
    out_ref, grad_ref,
    adj, sent, ring, plane, phys, visc, rows, back, fold, pencil, part, part_a, part_b,
    s1, r1, s2, r2, s3, r3, s4, r4, sv, rv, sa, ra,
):
    gy = lax.axis_index("gy")
    gz = lax.axis_index("gz")
    x = gz // 8
    z_lo = gz // 4 % 2
    y = gz % 4
    e = z_lo * 4 + gy
    w = x * 4 + y

    def ring_id(other):
        return {"gy": other % 4, "gz": x * 8 + other // 4 * 4 + y}

    def sheet_id(other):
        return {"gy": gy, "gz": other // 4 * 8 + z_lo * 4 + other % 4}

    def to_ring(step):
        return (e + step) % RING

    def to_sheet(step):
        return (w + step) % RINGS

    barrier = pltpu.get_barrier_semaphore()

    @pl.loop(1, RING)
    def _(step):
        pl.semaphore_signal(barrier, inc=1, device_id=ring_id(to_ring(step)), device_id_type=MESH)

    @pl.loop(1, RINGS)
    def _(step):
        pl.semaphore_signal(barrier, inc=1, device_id=sheet_id(to_sheet(step)), device_id_type=MESH)

    pl.semaphore_wait(barrier, RING + RINGS - 2)

    def exchange(steps, target, device, source, landing, send, receive):
        @pl.loop(1, steps)
        def _(step):
            other = target(step)
            pltpu.make_async_remote_copy(
                src_ref=source(other), dst_ref=landing, send_sem=send, recv_sem=receive,
                device_id=device(other), device_id_type=MESH,
            ).start()

        pltpu.make_async_copy(source(target(0)), landing, receive).start()

    def drain(ref, sem):
        pltpu.make_async_copy(ref, ref, sem).wait()

    def lanes(index):
        return pl.ds(pl.multiple_of(index * 128, 128), 128)

    def octet(index):
        return pl.ds(pl.multiple_of(index * 8, 8), 8)

    def send_visc():
        landing = visc.at[pl.ds(pl.multiple_of(gy * 64, 64), 64)]

        @pl.loop(1, 4)
        def _(step):
            other = (gy + step) % 4
            pltpu.make_async_remote_copy(
                src_ref=visc_ref.at[other], dst_ref=landing, send_sem=sv.at[0], recv_sem=rv.at[0],
                device_id={"gy": other, "gz": gz}, device_id_type=MESH,
            ).start()

        pltpu.make_async_copy(visc_ref.at[gy], landing, rv.at[0]).start()

    def send_ring(f):
        exchange(
            RING, to_ring, ring_id, lambda k: sent.at[f, k],
            ring.at[f, :, octet(z_lo), lanes(gy)], s1.at[f], r1.at[f],
        )

    def send_sheet(f):
        drain(ring.at[f], r1.at[f])
        slot = jnp.where(f < 5, f, f + 1)
        exchange(
            RINGS, to_sheet, sheet_id, lambda k: ring.at[f, k],
            plane.at[slot, w], s2.at[f], r2.at[f],
        )

    def z_inverse(source, f, base):
        table = (zi_ref[0], zi_ref[1])
        view = sent.reshape(10, 1024, 128)
        for pair in range(4):
            wide = []
            for ky in (2 * pair, 2 * pair + 1):
                own = source[f, pl.ds(ky, 128, stride=8), :]
                wide.append(jnp.concatenate([own, jnp.concatenate([-own[64:], own[:64]], 0)], 1))
            done = three(table, halves(jnp.concatenate(wide, 0)), dot_nt)
            for k in range(2):
                at = pl.ds(2 * pair + k, 128, stride=8)
                view[base + f, at, :] = done[:128, k * 128 : k * 128 + 128]

                @pl.when(f < 2)
                def _():
                    view[base + 3 + f, at, :] = done[128:, k * 128 : k * 128 + 128]

    def z_fields(source, base):
        @pl.loop(0, 3)
        def _(f):
            z_inverse(source, f, base)
            send_ring(base + f)

            @pl.when(f < 2)
            def _():
                send_ring(base + 3 + f)

    z_fields(modes_ref, 0)
    send_visc()

    def tile_waves(kx):
        wave_x = (2.0 * math.pi / NX) * (gy * WIDTH + kx).astype(F32)
        iy = gz * 8 + lax.broadcasted_iota(jnp.int32, (8, 128), 0)
        iz = lax.broadcasted_iota(jnp.int32, (8, 128), 1)
        wave_y = (2.0 * math.pi / NY) * jnp.where(iy < NY // 2, iy, iy - NY).astype(F32)
        wave_z = (2.0 * math.pi / NZ) * jnp.where(iz < NZ // 2, iz, iz - NZ).astype(F32)
        return wave_x, wave_y, wave_z

    @pl.loop(0, WIDTH)
    def _(kx):
        wave_x, wave_y, wave_z = tile_waves(kx)
        square = wave_x * wave_x + wave_y * wave_y + wave_z * wave_z
        inverse = jnp.where(square > 0, 1.0, 0.0) / jnp.where(square > 0, square, 1.0)
        first = octet(kx)
        scale = mask_ref[first, :].astype(F32) * jnp.where(gy * WIDTH + kx == 0, 1.0, 0.5)
        for c in range(2):
            at = octet(c * WIDTH + kx)
            v0, v1, v2 = cot_ref[0, at, :], cot_ref[1, at, :], cot_ref[2, at, :]
            along = (wave_x * v0 + wave_y * v1 + wave_z * v2) * inverse
            adj[0, at, :] = scale * (v0 - wave_x * along)
            adj[1, at, :] = scale * (v1 - wave_y * along)
            adj[2, at, :] = scale * (v2 - wave_z * along)

    z_fields(adj, 5)

    @pl.loop(0, 5)
    def _(f):
        send_sheet(f)

    lane = lax.broadcasted_iota(jnp.int32, (1, NX), 1)
    wave_x = (2.0 * math.pi / NX) * ((lane // 128) * WIDTH + lane % WIDTH).astype(F32)
    sign = jnp.where(lane % 128 < WIDTH, -1.0, 1.0).astype(F32)

    def turn(value):
        parts = [pltpu.roll(value[:, k * 128 : k * 128 + 128], 64, 1) for k in range(value.shape[1] // 128)]
        return jnp.concatenate(parts, 1) * sign[:, : value.shape[1]]

    def wave_y_of(block):
        row = lax.broadcasted_iota(jnp.int32, (16, 1), 0)
        mode = (block // 4) * 64 + (block % 4) * 8 + (row // 8) * 32 + row % 8
        return (2.0 * math.pi / NY) * jnp.where(mode < NY // 2, mode, mode - NY).astype(F32)

    def to_cells(group, j):
        index = group * 6 + j
        for h in range(2):
            cols = pl.ds(h * 256, 256)
            both = three((yi_ref[0], yi_ref[1]), halves(plane[index, :, :, cols].reshape(NY, 256)))
            rows[:, cols] = both[:NY] + turn(both[NY:])
        moved = halves(rows[...])
        for h in range(2):
            cols = pl.ds(h * 256, 256)
            done = three(moved, (xi_ref[0, :, cols], xi_ref[1, :, cols]))
            phys[index, :, cols] = done

    @pl.loop(0, 2)
    def _(group):
        @pl.loop(0, 5)
        def _(j):
            drain(plane.at[group * 6 + j], r2.at[group * 5 + j])

        base = group * 6

        @pl.loop(0, RINGS)
        def _(block):
            wave_y = wave_y_of(block)
            t0, t1, t2 = [turn(plane[base + k, block]) for k in range(3)]
            d0, d1 = plane[base + 3, block], plane[base + 4, block]
            plane[base + 3, block] = d0 - wave_x * t2
            plane[base + 4, block] = wave_y * t2 - d1
            plane[base + 5, block] = wave_x * t1 - wave_y * t0

        @pl.loop(0, 6)
        def _(j):
            to_cells(group, j)

            @pl.when((group == 0) & (j < 5))
            def _():
                send_sheet(5 + j)

    hub_x, hub_y, hub_z = turb_ref[0:1, :], turb_ref[1:2, :], turb_ref[2:3, :]
    normal_x, normal_y, thrust = turb_ref[3:4, :], turb_ref[4:5, :], turb_ref[5:6, :]
    cell_x = lax.broadcasted_iota(jnp.int32, (NX, 128), 0).astype(F32)
    hot = jnp.where(cell_x == hub_x, 1.0, 0.0).astype(BF16)
    off_y = lax.broadcasted_iota(jnp.int32, (NY, 128), 0).astype(F32) - hub_y
    off_z = (gz * 4 + gy).astype(F32) - hub_z
    disk = jnp.where(off_y * off_y + off_z * off_z <= float(RADIUS * RADIUS), 1.0, 0.0)

    def project(first, inflow):
        def column(index, mean):
            high, low = halves(phys[index] + mean)
            return dot(high, hot) + dot(low, hot)

        mixed = normal_x * column(first, inflow[0]) + normal_y * column(first + 1, inflow[1])
        return jnp.sum(disk * mixed, axis=0, keepdims=True)

    part[...] = jnp.zeros((8, 128), F32)
    part[0:1, :] = project(0, (inflow_ref[0], inflow_ref[1]))
    part[1:2, :] = project(6, (0.0, 0.0))
    exchange(RING, to_ring, ring_id, lambda k: part, part_a.at[e], sa.at[0], ra.at[0])
    drain(visc, rv.at[0])

    @pl.loop(0, 32)
    def _(block):
        at = octet(block)
        u0, u1, u2 = [phys[k, at] + inflow_ref[k] for k in range(3)]
        w1, w0, w2 = [phys[3 + k, at] for k in range(3)]
        p0, p1, p2 = [phys[6 + k, at] for k in range(3)]
        q1, q0, q2 = [phys[9 + k, at] for k in range(3)]
        nu = visc[at]
        phys[0, at] = p1 * u2 - p2 * u1 - nu * q0
        phys[1, at] = p2 * u0 - p0 * u2 - nu * q1
        phys[2, at] = p0 * u1 - p1 * u0 - nu * q2
        phys[3, at] = w1 * p2 - w2 * p1
        phys[4, at] = w2 * p0 - w0 * p2
        phys[5, at] = w0 * p1 - w1 * p0

    drain(part_a, ra.at[0])
    total = part_a[0]
    for k in range(1, RING):
        total = total + part_a[k]
    part_b[RINGS] = total
    exchange(RINGS, to_sheet, sheet_id, lambda k: part_b.at[RINGS], part_b.at[w], sa.at[1], ra.at[1])

    def add_force():
        drain(part_b.at[pl.ds(0, RINGS)], ra.at[1])
        total = part_b[0]
        for k in range(1, RINGS):
            total = total + part_b[k]
        disk_speed = total[0:1] / disk_area()
        push = total[1:2]
        grad_ref[...] = jnp.broadcast_to(-0.5 * SECTION_STEP * disk_speed * jnp.abs(disk_speed) * push, (8, 128))
        weight = -thrust * jnp.abs(disk_speed) * push / disk_area()
        for index, normal in ((3, normal_x), (4, normal_y)):
            high, low = halves(disk * (weight * normal))
            phys[index] = phys[index] + dot_nt(high, hot) + dot_nt(low, hot)

    def send_back(k):
        exchange(
            RINGS, to_sheet, sheet_id, lambda other: back.at[k, other],
            fold.at[k, w], s3.at[k], r3.at[k],
        )

    def send_home(k):
        drain(fold.at[k], r3.at[k])
        exchange(
            RING, to_ring, ring_id, lambda other: fold.at[k, :, octet(other // 4), lanes(other % 4)],
            pencil.at[k, e], s4.at[k], r4.at[k],
        )

    @pl.loop(0, 6)
    def _(j):
        @pl.when(j == 3)
        def _():
            add_force()

        moved = halves(phys[j])
        for h in range(2):
            cols = pl.ds(h * 256, 256)
            spectrum = three(moved, (xf_ref[0, :, cols], xf_ref[1, :, cols]))
            both = three((yf_ref[0], yf_ref[1]), halves(spectrum))
            plane[j, :, :, cols] = (both[:NY] - turn(both[NY:])).reshape(RINGS, 16, 256)

        @pl.loop(0, RINGS)
        def _(block):
            own = plane[j, block]

            @pl.when(j < 2)
            def _():
                back[j, block] = own

            @pl.when(j == 3)
            def _():
                back[2, block] = own + wave_y_of(block) * turn(plane[2, block])

            @pl.when(j == 4)
            def _():
                back[3, block] = own - wave_x * turn(plane[2, block])

            @pl.when(j == 5)
            def _():
                back[4, block] = own + wave_x * turn(plane[1, block]) - wave_y_of(block) * turn(plane[0, block])

        @pl.when(j < 2)
        def _():
            send_back(j)

        @pl.when(j > 2)
        def _():
            send_back(j - 1)

        @pl.when((j == 2) | (j == 3))
        def _():
            send_home(j - 2)

        @pl.when(j > 3)
        def _():
            send_home(j - 2)

    send_home(4)

    @pl.loop(0, 5)
    def _(k):
        drain(pencil.at[k], r4.at[k])

    pencils = pencil.reshape(5, 1024, 128)

    def z_forward(f, table, fields):
        for pair in range(4):
            tall = []
            for k in fields:
                own = jnp.concatenate([pencils[k, pl.ds(2 * pair + i, 128, stride=8), :] for i in range(2)], 1)
                tall += [own, turn(own)]
            done = three(table, halves(jnp.concatenate(tall, 0)))
            for i in range(2):
                at = pl.ds(2 * pair + i, 128, stride=8)
                doubled = jnp.where(
                    (lax.broadcasted_iota(jnp.int32, (128, 1), 0) % WIDTH == 0) & (gy == 0), 1.0, 2.0
                )
                out_ref[f, at, :] = adj[f, at, :] * doubled + SECTION_STEP * done[:, i * 128 : i * 128 + 128].T

    z_forward(0, (zf_ref[0, 0], zf_ref[1, 0]), (2, 1))
    z_forward(1, (zf_ref[0, 1], zf_ref[1, 1]), (3, 0))
    z_forward(2, (zf_ref[0, 0, :, :256], zf_ref[1, 0, :, :256]), (4,))

    @pl.loop(0, 10)
    def _(f):
        drain(sent.at[f, pl.ds(0, RING - 1)], s1.at[f])
        drain(ring.at[f, pl.ds(0, RINGS - 1)], s2.at[f])

    @pl.loop(0, 5)
    def _(k):
        drain(back.at[k, pl.ds(0, RINGS - 1)], s3.at[k])
        drain(pencil.at[k, pl.ds(0, RING - 1)], s4.at[k])

    drain(visc.at[pl.ds(0, 192)], sv.at[0])
    drain(part_a.at[pl.ds(0, RING - 1)], sa.at[0])
    drain(part_b.at[pl.ds(0, RINGS - 1)], sa.at[1])


def local(velocity_hat, inflow, viscosity, cot_hat, mode_mask, hub_cells, yaw_sector, thrust):
    count = thrust.shape[0]
    angle = (yaw_sector.astype(F32) - 6.0) * (math.pi / 36.0)
    hubs = hub_cells.astype(F32)
    turbines = jnp.stack([hubs[:, 0], hubs[:, 1], hubs[:, 2], jnp.cos(angle), jnp.sin(angle), thrust, thrust, thrust])
    turbines = jnp.pad(turbines, ((0, 0), (0, 128 - count)), constant_values=-1000.0)
    vmem = pl.BlockSpec(memory_space=pltpu.VMEM)
    smem = pl.BlockSpec(memory_space=pltpu.SMEM)
    dma = pltpu.SemaphoreType.DMA
    adjoint, grad = pl.pallas_call(
        kernel,
        out_shape=(
            jax.ShapeDtypeStruct((3, 1024, 128), F32),
            jax.ShapeDtypeStruct((8, 128), F32),
        ),
        in_specs=[vmem, smem] + [vmem] * 10,
        out_specs=(vmem, vmem),
        scratch_shapes=[
            pltpu.VMEM((3, 1024, 128), F32),
            pltpu.VMEM((10, RING, RINGS, 8, 128), F32),
            pltpu.VMEM((10, RINGS, 16, NX), F32),
            pltpu.VMEM((12, RINGS, 16, NX), F32),
            pltpu.VMEM((12, NY, NX), F32),
            pltpu.VMEM((NY, NX), F32),
            pltpu.VMEM((NY, NX), F32),
            pltpu.VMEM((5, RINGS, 16, NX), F32),
            pltpu.VMEM((5, RINGS, 16, NX), F32),
            pltpu.VMEM((5, RING, RINGS, 8, 128), F32),
            pltpu.VMEM((8, 128), F32),
            pltpu.VMEM((RING, 8, 128), F32),
            pltpu.VMEM((RINGS + 1, 8, 128), F32),
            dma((10,)), dma((10,)), dma((10,)), dma((10,)),
            dma((5,)), dma((5,)), dma((5,)), dma((5,)),
            dma((1,)), dma((1,)), dma((2,)), dma((2,)),
        ],
        compiler_params=pltpu.CompilerParams(
            collective_id=0, has_side_effects=True, vmem_limit_bytes=60 * 1024 * 1024
        ),
    )(
        velocity_hat.reshape(3, 1024, 128),
        inflow,
        viscosity,
        cot_hat.reshape(3, 1024, 128),
        mode_mask.reshape(512, 128),
        turbines,
        *[jnp.asarray(t) for t in tables()],
    )
    return adjoint.reshape(velocity_hat.shape), grad[0, :count]


def solution(mesh):
    placed = (
        P(None, None, "gy", "gz", None),
        P(),
        P("gz", "gy", None),
        P(None, None, "gy", "gz", None),
        P("gy", "gz", None),
        P(),
        P(),
        P(),
    )
    return jax.shard_map(
        local,
        mesh=mesh,
        in_specs=placed,
        out_specs=(P(None, None, "gy", "gz", None), P()),
        check_vma=False,
    )
```

time: 488 us -> 169 us (0.35)
  Pallas kernels: 0 us -> 159 us
  blocking collectives: 150 us -> 0 us
  local copies, waits for them, and re-layouts: 133 us -> 5.23 us
  matrix products: 65.8 us -> 0 us
  waiting for transfers between devices: 64.6 us -> 0 us
  starting transfers between devices: 35.4 us -> 0 us
  other arithmetic: 32.7 us -> 1.39 us
    pallas_call x0 -> x1, Pallas kernels: none -> 159 us  [local(): pl.pallas_call(kernel, out_shape=(jax.ShapeDtypeStruct((3, 1024, 128), F3...]
    all_to_all x2 -> x0, blocking collectives: 85.4 us -> none  [the longest x1 43.1 us: local(): lax.all_to_all(columns, 'gz', split_axis=2, concat_axis=1, tiled=True)]
    reshape x12 -> x0, local copies, waits for them, and re-layouts: 70.3 us -> none  [the longest x4 33.1 us: y_inverse(): columns.reshape(columns.shape[0], columns.shape[1], columns.shape[2], 2,...]
    dot_general x14 -> x0, matrix products: 65.8 us -> none  [the longest x2 15.3 us: y_inverse(): moved = jnp.einsum('fzbra,rbsy->fzysa', halves, table_y, precision=PRECISE)]
    psum x1 -> x0, blocking collectives: 64.9 us -> none  [local(): lax.psum((disk_project(velocity, normal, along_x, disk), disk_project(pul...]
    all_to_all x4 -> x0, waiting for transfers between devices: 64.6 us -> none  [the longest x2 41 us: to_physical(): lax.all_to_all(z_inverse(spectrum, table_z), 'gz', split_axis=1, concat_a...]
    all_to_all x4 -> x0, starting transfers between devices: 35.4 us -> none  [the longest x2 25.7 us: to_physical(): lax.all_to_all(z_inverse(spectrum, table_z), 'gz', split_axis=1, concat_a...]
    unnamed x47 -> x1, local copies, waits for them, and re-layouts: 27 us -> 2.65 us
  transfers between devices with their start and end apart: 4 -> 0, of which waited for: 4 -> 0; matrix products, arithmetic and copies ran while one was open for 20% -> 0% of each run, Pallas kernels for 0% -> 0%
where the time goes in v1:
time: 169 us; the launch traced here: 166 us
  Pallas kernels  159 us (94%)
  local copies, waits for them, and re-layouts  5.23 us (3%)
    pallas_call x1, Pallas kernels, local(): pl.pallas_call(kernel, out_shape=(jax.ShapeDtypeStruct((3, 1024, 128), F3...  159 us

profile of v1, /device:TPU:0, one launch (start us, length us, event | category | flops | bytes accessed | tf_op | source)
XLA Modules:
  0.0 166.5 jit_solution(15562485299575289714)
XLA Ops:
  0.6 0.7 sine_bitcast_fusion
  1.3 0.7 convert_element_type.6
  2.0 0.8 stack.17
  2.8 0.6 pad.4.turb_ref
  3.4 159.2 %shard_map.149 = (f32[3,1024,128]{2,1,0:T(8,128)}, f32[8,128]{1,0:T(8,128)}) custom-call(f32[3,1024,128]{2,1,0:T(8,128)} %bitcast.17, f32[3]{0:T(128)} %inflow_ref.1, f32[4,64,512]{2,1,0:T(8,128)} %visc_ref.1, f32[3,1024,128]{2,1,0:T(8,128)} %bitcast.18, s32[512,128]{1,0:T(8,128)} %bitcast.20, f32[8,128]{1,0:T(8,128)} %pad.4.turb_ref, ...), custom_call_target="tpu_custom_call" | custom-call | tf_op jit(solution)/shard_map/pallas_call | solution.py:446
  162.6 1.2 slice_bitcast_fusion
  163.8 2.7 %copy.17 = f32[3,2,64,8,128]{4,3,2,1,0:T(8,128)} copy(f32[3,2,64,8,128]{4,3,2,1,0:T(8,128)} %bitcast.19) | data formatting | bytes 3145728
  (1 shorter events, 0.0 us)

commit v2 on v1

--- a/solution.py
+++ b/solution.py
@@ -83,7 +83,7 @@
     modes_ref, inflow_ref, visc_ref, cot_ref, mask_ref, turb_ref,
     zi_ref, zf_ref, yi_ref, yf_ref, xi_ref, xf_ref,
     out_ref, grad_ref,
-    adj, sent, ring, plane, phys, visc, rows, back, fold, pencil, part, part_a, part_b,
+    adj, sent, ring, sheet, plane, phys, visc, rows, fold, turned, pencil, part, part_a, part_b,
     s1, r1, s2, r2, s3, r3, s4, r4, sv, rv, sa, ra,
 ):
     gy = lax.axis_index("gy")
@@ -91,8 +91,12 @@
     x = gz // 8
     z_lo = gz // 4 % 2
     y = gz % 4
+    z = gy // 2 * 2 + z_lo
+    core = gy % 2
     e = z_lo * 4 + gy
     w = x * 4 + y
+    kept_x = gy < 3
+    kept = kept_x & ((gz < 11) | (gz > 20))
 
     def ring_id(other):
         return {"gy": other % 4, "gz": x * 8 + other // 4 * 4 + y}
@@ -101,10 +105,13 @@
         return {"gy": gy, "gz": other // 4 * 8 + z_lo * 4 + other % 4}
 
     def to_ring(step):
-        return (e + step) % RING
+        turn = step * 3 % RING
+        there = (z + turn) % 4
+        return there % 2 * 4 + there // 2 * 2 + (core + turn // 4) % 2
 
     def to_sheet(step):
-        return (w + step) % RINGS
+        turn = step * 5 % RINGS
+        return (x + turn // 4) % 4 * 4 + (y + turn) % 4
 
     barrier = pltpu.get_barrier_semaphore()
 
@@ -129,71 +136,37 @@
 
         pltpu.make_async_copy(source(target(0)), landing, receive).start()
 
+    def to_rings(source, landing, send, receive):
+        exchange(RING, to_ring, ring_id, source, landing, send, receive)
+
+    def to_sheets(source, landing, send, receive):
+        exchange(RINGS, to_sheet, sheet_id, source, landing, send, receive)
+
     def drain(ref, sem):
         pltpu.make_async_copy(ref, ref, sem).wait()
 
+    tiles = sent.reshape(1280, 8, 128)
+
+    def drain_tiles(count, sem):
+        drain(tiles.at[pl.ds(0, count)], sem)
+
     def lanes(index):
         return pl.ds(pl.multiple_of(index * 128, 128), 128)
 
     def octet(index):
         return pl.ds(pl.multiple_of(index * 8, 8), 8)
 
-    def send_visc():
-        landing = visc.at[pl.ds(pl.multiple_of(gy * 64, 64), 64)]
-
-        @pl.loop(1, 4)
-        def _(step):
-            other = (gy + step) % 4
-            pltpu.make_async_remote_copy(
-                src_ref=visc_ref.at[other], dst_ref=landing, send_sem=sv.at[0], recv_sem=rv.at[0],
-                device_id={"gy": other, "gz": gz}, device_id_type=MESH,
-            ).start()
-
-        pltpu.make_async_copy(visc_ref.at[gy], landing, rv.at[0]).start()
-
-    def send_ring(f):
-        exchange(
-            RING, to_ring, ring_id, lambda k: sent.at[f, k],
-            ring.at[f, :, octet(z_lo), lanes(gy)], s1.at[f], r1.at[f],
-        )
-
-    def send_sheet(f):
-        drain(ring.at[f], r1.at[f])
-        slot = jnp.where(f < 5, f, f + 1)
-        exchange(
-            RINGS, to_sheet, sheet_id, lambda k: ring.at[f, k],
-            plane.at[slot, w], s2.at[f], r2.at[f],
-        )
-
-    def z_inverse(source, f, base):
-        table = (zi_ref[0], zi_ref[1])
-        view = sent.reshape(10, 1024, 128)
-        for pair in range(4):
-            wide = []
-            for ky in (2 * pair, 2 * pair + 1):
-                own = source[f, pl.ds(ky, 128, stride=8), :]
-                wide.append(jnp.concatenate([own, jnp.concatenate([-own[64:], own[:64]], 0)], 1))
-            done = three(table, halves(jnp.concatenate(wide, 0)), dot_nt)
-            for k in range(2):
-                at = pl.ds(2 * pair + k, 128, stride=8)
-                view[base + f, at, :] = done[:128, k * 128 : k * 128 + 128]
-
-                @pl.when(f < 2)
-                def _():
-                    view[base + 3 + f, at, :] = done[128:, k * 128 : k * 128 + 128]
-
-    def z_fields(source, base):
-        @pl.loop(0, 3)
-        def _(f):
-            z_inverse(source, f, base)
-            send_ring(base + f)
-
-            @pl.when(f < 2)
-            def _():
-                send_ring(base + 3 + f)
-
-    z_fields(modes_ref, 0)
-    send_visc()
+    landing = visc.at[pl.ds(pl.multiple_of(gy * 64, 64), 64)]
+
+    @pl.loop(1, 4)
+    def _(step):
+        other = (gy + step) % 4
+        pltpu.make_async_remote_copy(
+            src_ref=visc_ref.at[other], dst_ref=landing, send_sem=sv.at[0], recv_sem=rv.at[0],
+            device_id={"gy": other, "gz": gz}, device_id_type=MESH,
+        ).start()
+
+    pltpu.make_async_copy(visc_ref.at[gy], landing, rv.at[0]).start()
 
     def tile_waves(kx):
         wave_x = (2.0 * math.pi / NX) * (gy * WIDTH + kx).astype(F32)
@@ -218,11 +191,76 @@
             adj[1, at, :] = scale * (v1 - wave_y * along)
             adj[2, at, :] = scale * (v2 - wave_z * along)
 
-    z_fields(adj, 5)
-
-    @pl.loop(0, 5)
+    def z_inverse(source, f, base):
+        table = (zi_ref[0], zi_ref[1])
+        view = sent.reshape(10, 1024, 128)
+        for pair in range(4):
+            wide = []
+            for ky in (2 * pair, 2 * pair + 1):
+                own = source[f, pl.ds(ky, 128, stride=8), :]
+                wide.append(jnp.concatenate([own, jnp.concatenate([-own[64:], own[:64]], 0)], 1))
+            done = three(table, halves(jnp.concatenate(wide, 0)), dot_nt)
+            for k in range(2):
+                at = pl.ds(2 * pair + k, 128, stride=8)
+                view[base + f, at, :] = done[:128, k * 128 : k * 128 + 128]
+
+                @pl.when(f < 2)
+                def _():
+                    view[base + 3 + f, at, :] = done[128:, k * 128 : k * 128 + 128]
+
+    def flow_first(f):
+        to_rings(lambda k: sent.at[f, k], ring.at[f, :, octet(z_lo), lanes(gy)], s1.at[f], r1.at[f])
+
+    def flow_second(f):
+        drain(ring.at[f], r1.at[f])
+        to_sheets(lambda k: ring.at[f, k], plane.at[f, w], s2.at[f], r2.at[f])
+
+    def pull_first(f):
+        to_sheets(lambda k: sent.at[f, :, k], sheet.at[f - 5, w], s1.at[f], r1.at[f])
+
+    def pull_second(f):
+        @pl.when(kept_x)
+        def _():
+            drain_tiles(88, r1.at[f])
+            for first, count in ((0, 4), (4 + 5 * z_lo, 3), (12, 4)):
+                some = pl.ds(first, count)
+                to_rings(
+                    lambda k: sheet.at[f - 5, some, k], plane.at[f + 1, some, octet(z_lo), lanes(gy)],
+                    s2.at[f], r2.at[f],
+                )
+
+    @pl.loop(0, 3)
     def _(f):
-        send_sheet(f)
+        @pl.when(kept)
+        def _():
+            z_inverse(adj, f, 5)
+            pull_first(5 + f)
+
+            @pl.when(f < 2)
+            def _():
+                pull_first(8 + f)
+
+    @pl.loop(0, 3)
+    def _(f):
+        z_inverse(modes_ref, f, 0)
+        flow_first(f)
+
+    @pl.loop(6, 11)
+    def _(slot):
+        plane[slot, :, :, 384:] = jnp.zeros((RINGS, 16, 128), F32)
+        plane[slot, 4:7, 8:, :384] = jnp.zeros((3, 8, 384), F32)
+        plane[slot, 7:9, :, :384] = jnp.zeros((2, 16, 384), F32)
+        plane[slot, 9:12, :8, :384] = jnp.zeros((3, 8, 384), F32)
+
+    @pl.loop(0, 3)
+    def _(f):
+        pull_second(5 + f)
+        flow_second(f)
+
+    @pl.loop(3, 5)
+    def _(f):
+        pull_second(5 + f)
+        flow_first(f)
 
     lane = lax.broadcasted_iota(jnp.int32, (1, NX), 1)
     wave_x = (2.0 * math.pi / NX) * ((lane // 128) * WIDTH + lane % WIDTH).astype(F32)
@@ -237,8 +275,17 @@
         mode = (block // 4) * 64 + (block % 4) * 8 + (row // 8) * 32 + row % 8
         return (2.0 * math.pi / NY) * jnp.where(mode < NY // 2, mode, mode - NY).astype(F32)
 
-    def to_cells(group, j):
-        index = group * 6 + j
+    def curl(base):
+        @pl.loop(0, RINGS)
+        def _(block):
+            wave_y = wave_y_of(block)
+            t0, t1, t2 = [turn(plane[base + k, block]) for k in range(3)]
+            d0, d1 = plane[base + 3, block], plane[base + 4, block]
+            plane[base + 3, block] = d0 - wave_x * t2
+            plane[base + 4, block] = wave_y * t2 - d1
+            plane[base + 5, block] = wave_x * t1 - wave_y * t0
+
+    def to_cells(index):
         for h in range(2):
             cols = pl.ds(h * 256, 256)
             both = three((yi_ref[0], yi_ref[1]), halves(plane[index, :, :, cols].reshape(NY, 256)))
@@ -249,30 +296,19 @@
             done = three(moved, (xi_ref[0, :, cols], xi_ref[1, :, cols]))
             phys[index, :, cols] = done
 
-    @pl.loop(0, 2)
-    def _(group):
-        @pl.loop(0, 5)
-        def _(j):
-            drain(plane.at[group * 6 + j], r2.at[group * 5 + j])
-
-        base = group * 6
-
-        @pl.loop(0, RINGS)
-        def _(block):
-            wave_y = wave_y_of(block)
-            t0, t1, t2 = [turn(plane[base + k, block]) for k in range(3)]
-            d0, d1 = plane[base + 3, block], plane[base + 4, block]
-            plane[base + 3, block] = d0 - wave_x * t2
-            plane[base + 4, block] = wave_y * t2 - d1
-            plane[base + 5, block] = wave_x * t1 - wave_y * t0
-
-        @pl.loop(0, 6)
-        def _(j):
-            to_cells(group, j)
-
-            @pl.when((group == 0) & (j < 5))
-            def _():
-                send_sheet(5 + j)
+    @pl.loop(5, 10)
+    def _(f):
+        drain_tiles(66, r2.at[f])
+
+    curl(6)
+
+    @pl.loop(0, 9)
+    def _(task):
+        @pl.when(task > 5)
+        def _():
+            drain(plane.at[task - 6], r2.at[task - 6])
+
+        to_cells((task + 6) % 12)
 
     hub_x, hub_y, hub_z = turb_ref[0:1, :], turb_ref[1:2, :], turb_ref[2:3, :]
     normal_x, normal_y, thrust = turb_ref[3:4, :], turb_ref[4:5, :], turb_ref[5:6, :]
@@ -293,112 +329,132 @@
     part[...] = jnp.zeros((8, 128), F32)
     part[0:1, :] = project(0, (inflow_ref[0], inflow_ref[1]))
     part[1:2, :] = project(6, (0.0, 0.0))
-    exchange(RING, to_ring, ring_id, lambda k: part, part_a.at[e], sa.at[0], ra.at[0])
+    to_rings(lambda k: part, part_a.at[e], sa.at[0], ra.at[0])
+    flow_second(3)
     drain(visc, rv.at[0])
 
     @pl.loop(0, 32)
     def _(block):
         at = octet(block)
         u0, u1, u2 = [phys[k, at] + inflow_ref[k] for k in range(3)]
-        w1, w0, w2 = [phys[3 + k, at] for k in range(3)]
         p0, p1, p2 = [phys[6 + k, at] for k in range(3)]
         q1, q0, q2 = [phys[9 + k, at] for k in range(3)]
         nu = visc[at]
-        phys[0, at] = p1 * u2 - p2 * u1 - nu * q0
-        phys[1, at] = p2 * u0 - p0 * u2 - nu * q1
-        phys[2, at] = p0 * u1 - p1 * u0 - nu * q2
-        phys[3, at] = w1 * p2 - w2 * p1
-        phys[4, at] = w2 * p0 - w0 * p2
-        phys[5, at] = w0 * p1 - w1 * p0
+        phys[9, at] = p1 * u2 - p2 * u1 - nu * q0
+        phys[10, at] = p2 * u0 - p0 * u2 - nu * q1
+        phys[11, at] = p0 * u1 - p1 * u0 - nu * q2
 
     drain(part_a, ra.at[0])
     total = part_a[0]
     for k in range(1, RING):
         total = total + part_a[k]
     part_b[RINGS] = total
-    exchange(RINGS, to_sheet, sheet_id, lambda k: part_b.at[RINGS], part_b.at[w], sa.at[1], ra.at[1])
-
-    def add_force():
-        drain(part_b.at[pl.ds(0, RINGS)], ra.at[1])
-        total = part_b[0]
-        for k in range(1, RINGS):
-            total = total + part_b[k]
-        disk_speed = total[0:1] / disk_area()
-        push = total[1:2]
-        grad_ref[...] = jnp.broadcast_to(-0.5 * SECTION_STEP * disk_speed * jnp.abs(disk_speed) * push, (8, 128))
-        weight = -thrust * jnp.abs(disk_speed) * push / disk_area()
-        for index, normal in ((3, normal_x), (4, normal_y)):
-            high, low = halves(disk * (weight * normal))
-            phys[index] = phys[index] + dot_nt(high, hot) + dot_nt(low, hot)
-
-    def send_back(k):
-        exchange(
-            RINGS, to_sheet, sheet_id, lambda other: back.at[k, other],
-            fold.at[k, w], s3.at[k], r3.at[k],
-        )
-
-    def send_home(k):
-        drain(fold.at[k], r3.at[k])
-        exchange(
-            RING, to_ring, ring_id, lambda other: fold.at[k, :, octet(other // 4), lanes(other % 4)],
-            pencil.at[k, e], s4.at[k], r4.at[k],
-        )
-
-    @pl.loop(0, 6)
-    def _(j):
-        @pl.when(j == 3)
-        def _():
-            add_force()
-
-        moved = halves(phys[j])
+    to_sheets(lambda k: part_b.at[RINGS], part_b.at[w], sa.at[1], ra.at[1])
+
+    def to_modes(source, target):
+        moved = halves(phys[source])
         for h in range(2):
             cols = pl.ds(h * 256, 256)
             spectrum = three(moved, (xf_ref[0, :, cols], xf_ref[1, :, cols]))
             both = three((yf_ref[0], yf_ref[1]), halves(spectrum))
-            plane[j, :, :, cols] = (both[:NY] - turn(both[NY:])).reshape(RINGS, 16, 256)
+            plane[target, :, :, cols] = (both[:NY] - turn(both[NY:])).reshape(RINGS, 16, 256)
+
+    def mine(ref, k):
+        return ref.at[:, octet(k // 4), lanes(k % 4)]
+
+    def even_first(k, slot):
+        to_sheets(lambda other: plane.at[slot, other], fold.at[k // 2, w], s3.at[k], r3.at[k])
+
+    def even_second(k):
+        drain(fold.at[k // 2], r3.at[k])
+        to_rings(lambda other: mine(fold.at[k // 2], other), pencil.at[k, e], s4.at[k], r4.at[k])
+
+    def odd_first(k, slot):
+        to_rings(lambda other: mine(plane.at[slot], other), turned.at[k // 2, e], s3.at[k], r3.at[k])
+
+    def odd_second(k):
+        drain(turned.at[k // 2], r3.at[k])
+        to_sheets(lambda other: turned.at[k // 2, :, other], pencil.at[k, :, w], s4.at[k], r4.at[k])
+
+    @pl.loop(0, 3)
+    def _(j):
+        to_modes(9 + j, 6 + j)
+
+        @pl.when(j == 0)
+        def _():
+            even_first(0, 6)
+            flow_second(4)
+
+        @pl.when(j == 1)
+        def _():
+            odd_first(1, 7)
+
+    drain(plane.at[3], r2.at[3])
+    drain(plane.at[4], r2.at[4])
+    curl(0)
+
+    @pl.loop(3, 6)
+    def _(index):
+        to_cells(index)
+
+    @pl.loop(0, 32)
+    def _(block):
+        at = octet(block)
+        w1, w0, w2 = [phys[3 + k, at] for k in range(3)]
+        p0, p1, p2 = [phys[6 + k, at] for k in range(3)]
+        phys[3, at] = w1 * p2 - w2 * p1
+        phys[4, at] = w2 * p0 - w0 * p2
+        phys[5, at] = w0 * p1 - w1 * p0
+
+    drain(part_b.at[pl.ds(0, RINGS)], ra.at[1])
+    total = part_b[0]
+    for k in range(1, RINGS):
+        total = total + part_b[k]
+    disk_speed = total[0:1] / disk_area()
+    push = total[1:2]
+    grad_ref[...] = jnp.broadcast_to(-0.5 * SECTION_STEP * disk_speed * jnp.abs(disk_speed) * push, (8, 128))
+    weight = -thrust * jnp.abs(disk_speed) * push / disk_area()
+    for index, normal in ((3, normal_x), (4, normal_y)):
+        high, low = halves(disk * (weight * normal))
+        phys[index] = phys[index] + dot_nt(high, hot) + dot_nt(low, hot)
+
+    @pl.loop(0, 3)
+    def _(j):
+        to_modes(3 + j, 9 + j)
 
         @pl.loop(0, RINGS)
         def _(block):
-            own = plane[j, block]
-
-            @pl.when(j < 2)
+            own = plane[9 + j, block]
+
+            @pl.when(j == 0)
             def _():
-                back[j, block] = own
-
-            @pl.when(j == 3)
+                plane[9, block] = own + wave_y_of(block) * turn(plane[8, block])
+
+            @pl.when(j == 1)
             def _():
-                back[2, block] = own + wave_y_of(block) * turn(plane[2, block])
-
-            @pl.when(j == 4)
+                plane[10, block] = own - wave_x * turn(plane[8, block])
+
+            @pl.when(j == 2)
             def _():
-                back[3, block] = own - wave_x * turn(plane[2, block])
-
-            @pl.when(j == 5)
-            def _():
-                back[4, block] = own + wave_x * turn(plane[1, block]) - wave_y_of(block) * turn(plane[0, block])
-
-        @pl.when(j < 2)
-        def _():
-            send_back(j)
-
-        @pl.when(j > 2)
-        def _():
-            send_back(j - 1)
-
-        @pl.when((j == 2) | (j == 3))
-        def _():
-            send_home(j - 2)
-
-        @pl.when(j > 3)
-        def _():
-            send_home(j - 2)
-
-    send_home(4)
-
-    @pl.loop(0, 5)
-    def _(k):
-        drain(pencil.at[k], r4.at[k])
-
+                plane[11, block] = own + wave_x * turn(plane[7, block]) - wave_y_of(block) * turn(plane[6, block])
+
+        @pl.when(j == 0)
+        def _():
+            even_first(2, 9)
+            odd_second(1)
+            even_second(0)
+
+        @pl.when(j == 1)
+        def _():
+            odd_first(3, 10)
+
+        @pl.when(j == 2)
+        def _():
+            even_first(4, 11)
+
+    even_second(2)
+    odd_second(3)
+    even_second(4)
     pencils = pencil.reshape(5, 1024, 128)
 
     def z_forward(f, table, fields):
@@ -415,19 +471,36 @@
                 )
                 out_ref[f, at, :] = adj[f, at, :] * doubled + SECTION_STEP * done[:, i * 128 : i * 128 + 128].T
 
+    for k in range(3):
+        drain(pencil.at[k], r4.at[k])
     z_forward(0, (zf_ref[0, 0], zf_ref[1, 0]), (2, 1))
+    drain(pencil.at[3], r4.at[3])
     z_forward(1, (zf_ref[0, 1], zf_ref[1, 1]), (3, 0))
+    drain(pencil.at[4], r4.at[4])
     z_forward(2, (zf_ref[0, 0, :, :256], zf_ref[1, 0, :, :256]), (4,))
 
-    @pl.loop(0, 10)
+    @pl.loop(0, 5)
     def _(f):
-        drain(sent.at[f, pl.ds(0, RING - 1)], s1.at[f])
-        drain(ring.at[f, pl.ds(0, RINGS - 1)], s2.at[f])
-
-    @pl.loop(0, 5)
-    def _(k):
-        drain(back.at[k, pl.ds(0, RINGS - 1)], s3.at[k])
-        drain(pencil.at[k, pl.ds(0, RING - 1)], s4.at[k])
+        drain_tiles(112, s1.at[f])
+        drain_tiles(120, s2.at[f])
+
+        @pl.when(kept)
+        def _():
+            drain_tiles(120, s1.at[5 + f])
+
+        @pl.when(kept_x)
+        def _():
+            drain_tiles(77, s2.at[5 + f])
+
+        @pl.when(f % 2 == 0)
+        def _():
+            drain_tiles(120, s3.at[f])
+            drain_tiles(112, s4.at[f])
+
+        @pl.when(f % 2 == 1)
+        def _():
+            drain_tiles(112, s3.at[f])
+            drain_tiles(120, s4.at[f])
 
     drain(visc.at[pl.ds(0, 192)], sv.at[0])
     drain(part_a.at[pl.ds(0, RING - 1)], sa.at[0])
@@ -454,13 +527,14 @@
         scratch_shapes=[
             pltpu.VMEM((3, 1024, 128), F32),
             pltpu.VMEM((10, RING, RINGS, 8, 128), F32),
-            pltpu.VMEM((10, RINGS, 16, NX), F32),
+            pltpu.VMEM((5, RINGS, 16, NX), F32),
+            pltpu.VMEM((5, RINGS, RING, 8, 128), F32),
             pltpu.VMEM((12, RINGS, 16, NX), F32),
             pltpu.VMEM((12, NY, NX), F32),
             pltpu.VMEM((NY, NX), F32),
             pltpu.VMEM((NY, NX), F32),
-            pltpu.VMEM((5, RINGS, 16, NX), F32),
-            pltpu.VMEM((5, RINGS, 16, NX), F32),
+            pltpu.VMEM((3, RINGS, 16, NX), F32),
+            pltpu.VMEM((2, RING, RINGS, 8, 128), F32),
             pltpu.VMEM((5, RING, RINGS, 8, 128), F32),
             pltpu.VMEM((8, 128), F32),
             pltpu.VMEM((RING, 8, 128), F32),

time: 169 us -> 149 us (0.88); the launches traced: 166 us -> 149 us
  Pallas kernels: 159 us -> 142 us
    pallas_call x1, Pallas kernels: 159 us -> 142 us  [local(): pl.pallas_call(kernel, out_shape=(jax.ShapeDtypeStruct((3, 1024, 128), F3...]
where the time goes in v2:
time: 149 us
  Pallas kernels  142 us (95%)
  local copies, waits for them, and re-layouts  5.23 us (4%)
    pallas_call x1, Pallas kernels, local(): pl.pallas_call(kernel, out_shape=(jax.ShapeDtypeStruct((3, 1024, 128), F3...  142 us

profile of v2, /device:TPU:0, one launch (start us, length us, event | category | flops | bytes accessed | tf_op | source)
XLA Modules:
  0.0 148.8 jit_solution(11234291643313530029)
XLA Ops:
  0.6 0.7 sine_bitcast_fusion
  1.3 0.7 convert_element_type.6
  2.0 0.8 stack.17
  2.8 0.6 pad.4.turb_ref
  3.4 141.5 %shard_map.149 = (f32[3,1024,128]{2,1,0:T(8,128)}, f32[8,128]{1,0:T(8,128)}) custom-call(f32[3,1024,128]{2,1,0:T(8,128)} %bitcast.17, f32[3]{0:T(128)} %inflow_ref.1, f32[4,64,512]{2,1,0:T(8,128)} %visc_ref.1, f32[3,1024,128]{2,1,0:T(8,128)} %bitcast.18, s32[512,128]{1,0:T(8,128)} %bitcast.20, f32[8,128]{1,0:T(8,128)} %pad.4.turb_ref, ...), custom_call_target="tpu_custom_call" | custom-call | tf_op jit(solution)/shard_map/pallas_call | solution.py:519
  144.9 1.2 slice_bitcast_fusion
  146.1 2.7 %copy.17 = f32[3,2,64,8,128]{4,3,2,1,0:T(8,128)} copy(f32[3,2,64,8,128]{4,3,2,1,0:T(8,128)} %bitcast.19) | data formatting | bytes 3145728
  (1 shorter events, 0.0 us)

commit v3 on v2

--- a/solution.py
+++ b/solution.py
@@ -80,12 +80,16 @@
 
 
 def kernel(
-    modes_ref, inflow_ref, visc_ref, cot_ref, mask_ref, turb_ref,
-    zi_ref, zf_ref, yi_ref, yf_ref, xi_ref, xf_ref,
-    out_ref, grad_ref,
-    adj, sent, ring, sheet, plane, phys, visc, rows, fold, turned, pencil, part, part_a, part_b,
-    s1, r1, s2, r2, s3, r3, s4, r4, sv, rv, sa, ra,
+    inflow_ref, turb_ref, visc_ref, *refs,
 ):
+    held, refs = refs[:9], refs[9:]
+    (out_ref, grad_ref), refs = refs[:2], refs[2:]
+    loaded, refs = refs[:9], refs[9:]
+    cot_ref, mask_ref, zi_ref, modes_ref, yi_ref, xi_ref, xf_ref, yf_ref, zf_ref = loaded
+    (
+        adj, sent, ring, sheet, plane, phys, visc, rows, fold, turned, pencil, part, part_a, part_b,
+        s1, r1, s2, r2, s3, r3, s4, r4, sv, rv, sa, ra, load,
+    ) = refs
     gy = lax.axis_index("gy")
     gz = lax.axis_index("gz")
     x = gz // 8
@@ -123,6 +127,9 @@
     def _(step):
         pl.semaphore_signal(barrier, inc=1, device_id=sheet_id(to_sheet(step)), device_id_type=MESH)
 
+    loads = [pltpu.make_async_copy(held[k], loaded[k], load.at[k]) for k in range(9)]
+    for copy in loads:
+        copy.start()
     pl.semaphore_wait(barrier, RING + RINGS - 2)
 
     def exchange(steps, target, device, source, landing, send, receive):
@@ -175,6 +182,9 @@
         wave_y = (2.0 * math.pi / NY) * jnp.where(iy < NY // 2, iy, iy - NY).astype(F32)
         wave_z = (2.0 * math.pi / NZ) * jnp.where(iz < NZ // 2, iz, iz - NZ).astype(F32)
         return wave_x, wave_y, wave_z
+
+    loads[0].wait()
+    loads[1].wait()
 
     @pl.loop(0, WIDTH)
     def _(kx):
@@ -229,6 +239,8 @@
                     s2.at[f], r2.at[f],
                 )
 
+    loads[2].wait()
+
     @pl.loop(0, 3)
     def _(f):
         @pl.when(kept)
@@ -239,6 +251,8 @@
             @pl.when(f < 2)
             def _():
                 pull_first(8 + f)
+
+    loads[3].wait()
 
     @pl.loop(0, 3)
     def _(f):
@@ -257,10 +271,12 @@
         pull_second(5 + f)
         flow_second(f)
 
-    @pl.loop(3, 5)
-    def _(f):
-        pull_second(5 + f)
-        flow_first(f)
+    pull_second(8)
+    pull_second(9)
+    flow_first(3)
+    flow_first(4)
+    for copy in loads[4:]:
+        copy.wait()
 
     lane = lax.broadcasted_iota(jnp.int32, (1, NX), 1)
     wave_x = (2.0 * math.pi / NX) * ((lane // 128) * WIDTH + lane % WIDTH).astype(F32)
@@ -275,15 +291,16 @@
         mode = (block // 4) * 64 + (block % 4) * 8 + (row // 8) * 32 + row % 8
         return (2.0 * math.pi / NY) * jnp.where(mode < NY // 2, mode, mode - NY).astype(F32)
 
-    def curl(base):
+    def curl(base, slots):
         @pl.loop(0, RINGS)
         def _(block):
             wave_y = wave_y_of(block)
-            t0, t1, t2 = [turn(plane[base + k, block]) for k in range(3)]
-            d0, d1 = plane[base + 3, block], plane[base + 4, block]
-            plane[base + 3, block] = d0 - wave_x * t2
-            plane[base + 4, block] = wave_y * t2 - d1
-            plane[base + 5, block] = wave_x * t1 - wave_y * t0
+            if 3 in slots:
+                plane[base + 3, block] = plane[base + 3, block] - wave_x * turn(plane[base + 2, block])
+            if 4 in slots:
+                plane[base + 4, block] = wave_y * turn(plane[base + 2, block]) - plane[base + 4, block]
+            if 5 in slots:
+                plane[base + 5, block] = wave_x * turn(plane[base + 1, block]) - wave_y * turn(plane[base, block])
 
     def to_cells(index):
         for h in range(2):
@@ -296,22 +313,40 @@
             done = three(moved, (xi_ref[0, :, cols], xi_ref[1, :, cols]))
             phys[index, :, cols] = done
 
-    @pl.loop(5, 10)
-    def _(f):
-        drain_tiles(66, r2.at[f])
-
-    curl(6)
-
     @pl.loop(0, 9)
     def _(task):
-        @pl.when(task > 5)
-        def _():
-            drain(plane.at[task - 6], r2.at[task - 6])
-
-        to_cells((task + 6) % 12)
+        @pl.when(task < 3)
+        def _():
+            drain_tiles(66, r2.at[5 + task])
+
+        @pl.when(task == 3)
+        def _():
+            drain(plane.at[0], r2.at[0])
+
+        @pl.when(task == 4)
+        def _():
+            drain_tiles(66, r2.at[8])
+            drain_tiles(66, r2.at[9])
+            curl(6, (3, 4, 5))
+
+        @pl.when(task == 7)
+        def _():
+            drain(plane.at[1], r2.at[1])
+
+        @pl.when(task == 8)
+        def _():
+            flow_second(3)
+            drain(plane.at[2], r2.at[2])
+
+        to_cells(jnp.where(task < 3, task + 6, jnp.where(task == 3, 0, jnp.where(task < 7, task + 5, task - 6))))
 
     hub_x, hub_y, hub_z = turb_ref[0:1, :], turb_ref[1:2, :], turb_ref[2:3, :]
-    normal_x, normal_y, thrust = turb_ref[3:4, :], turb_ref[4:5, :], turb_ref[5:6, :]
+    sector, thrust = turb_ref[3:4, :], turb_ref[4:5, :]
+    normal_x = normal_y = jnp.zeros((1, 128), F32)
+    for k in range(13):
+        angle = (k - 6) * math.pi / 36.0
+        normal_x = jnp.where(sector == float(k), math.cos(angle), normal_x)
+        normal_y = jnp.where(sector == float(k), math.sin(angle), normal_y)
     cell_x = lax.broadcasted_iota(jnp.int32, (NX, 128), 0).astype(F32)
     hot = jnp.where(cell_x == hub_x, 1.0, 0.0).astype(BF16)
     off_y = lax.broadcasted_iota(jnp.int32, (NY, 128), 0).astype(F32) - hub_y
@@ -330,7 +365,6 @@
     part[0:1, :] = project(0, (inflow_ref[0], inflow_ref[1]))
     part[1:2, :] = project(6, (0.0, 0.0))
     to_rings(lambda k: part, part_a.at[e], sa.at[0], ra.at[0])
-    flow_second(3)
     drain(visc, rv.at[0])
 
     @pl.loop(0, 32)
@@ -389,22 +423,16 @@
         def _():
             odd_first(1, 7)
 
+    curl(0, (5,))
+    to_cells(5)
     drain(plane.at[3], r2.at[3])
-    drain(plane.at[4], r2.at[4])
-    curl(0)
-
-    @pl.loop(3, 6)
-    def _(index):
-        to_cells(index)
+    curl(0, (3,))
+    to_cells(3)
 
     @pl.loop(0, 32)
     def _(block):
         at = octet(block)
-        w1, w0, w2 = [phys[3 + k, at] for k in range(3)]
-        p0, p1, p2 = [phys[6 + k, at] for k in range(3)]
-        phys[3, at] = w1 * p2 - w2 * p1
-        phys[4, at] = w2 * p0 - w0 * p2
-        phys[5, at] = w0 * p1 - w1 * p0
+        phys[9, at] = phys[3, at] * phys[8, at] - phys[5, at] * phys[7, at]
 
     drain(part_b.at[pl.ds(0, RINGS)], ra.at[1])
     total = part_b[0]
@@ -412,24 +440,45 @@
         total = total + part_b[k]
     disk_speed = total[0:1] / disk_area()
     push = total[1:2]
-    grad_ref[...] = jnp.broadcast_to(-0.5 * SECTION_STEP * disk_speed * jnp.abs(disk_speed) * push, (8, 128))
+    grad = -0.5 * SECTION_STEP * disk_speed * jnp.abs(disk_speed) * push
+    grad_ref[...] = grad[:, : grad_ref.shape[1]]
     weight = -thrust * jnp.abs(disk_speed) * push / disk_area()
-    for index, normal in ((3, normal_x), (4, normal_y)):
+
+    def add_force(index, normal):
         high, low = halves(disk * (weight * normal))
         phys[index] = phys[index] + dot_nt(high, hot) + dot_nt(low, hot)
 
-    @pl.loop(0, 3)
+    add_force(9, normal_x)
+    to_modes(9, 9)
+
+    @pl.loop(0, RINGS)
+    def _(block):
+        plane[9, block] = plane[9, block] + wave_y_of(block) * turn(plane[8, block])
+
+    even_first(2, 9)
+    odd_second(1)
+    drain(plane.at[4], r2.at[4])
+    curl(0, (4,))
+    to_cells(4)
+
+    @pl.loop(0, 32)
+    def _(block):
+        at = octet(block)
+        w1, w0, w2 = [phys[3 + k, at] for k in range(3)]
+        p0, p1, p2 = [phys[6 + k, at] for k in range(3)]
+        phys[10, at] = w2 * p0 - w0 * p2
+        phys[11, at] = w0 * p1 - w1 * p0
+
+    add_force(10, normal_y)
+
+    @pl.loop(1, 3)
     def _(j):
-        to_modes(3 + j, 9 + j)
+        to_modes(9 + j, 9 + j)
 
         @pl.loop(0, RINGS)
         def _(block):
             own = plane[9 + j, block]
 
-            @pl.when(j == 0)
-            def _():
-                plane[9, block] = own + wave_y_of(block) * turn(plane[8, block])
-
             @pl.when(j == 1)
             def _():
                 plane[10, block] = own - wave_x * turn(plane[8, block])
@@ -438,15 +487,10 @@
             def _():
                 plane[11, block] = own + wave_x * turn(plane[7, block]) - wave_y_of(block) * turn(plane[6, block])
 
-        @pl.when(j == 0)
-        def _():
-            even_first(2, 9)
-            odd_second(1)
+        @pl.when(j == 1)
+        def _():
+            odd_first(3, 10)
             even_second(0)
-
-        @pl.when(j == 1)
-        def _():
-            odd_first(3, 10)
 
         @pl.when(j == 2)
         def _():
@@ -509,22 +553,29 @@
 
 def local(velocity_hat, inflow, viscosity, cot_hat, mode_mask, hub_cells, yaw_sector, thrust):
     count = thrust.shape[0]
-    angle = (yaw_sector.astype(F32) - 6.0) * (math.pi / 36.0)
-    hubs = hub_cells.astype(F32)
-    turbines = jnp.stack([hubs[:, 0], hubs[:, 1], hubs[:, 2], jnp.cos(angle), jnp.sin(angle), thrust, thrust, thrust])
-    turbines = jnp.pad(turbines, ((0, 0), (0, 128 - count)), constant_values=-1000.0)
+    row = lax.broadcasted_iota(jnp.int32, (8, 128), 0)
+    turbines = jnp.zeros((8, 128), F32)
+    columns = [hub_cells[:, 0], hub_cells[:, 1], hub_cells[:, 2], yaw_sector, thrust]
+    for k, column in enumerate(columns):
+        padded = jnp.pad(column.astype(F32), (0, 128 - count), constant_values=-1000.0)
+        turbines = jnp.where(row == k, padded[None, :], turbines)
     vmem = pl.BlockSpec(memory_space=pltpu.VMEM)
     smem = pl.BlockSpec(memory_space=pltpu.SMEM)
     dma = pltpu.SemaphoreType.DMA
+    z_inverse, z_forward, y_inverse, y_forward, x_inverse, x_forward = [jnp.asarray(t) for t in tables()]
+    operands = [
+        cot_hat.reshape(3, 1024, 128), mode_mask.reshape(512, 128), z_inverse, velocity_hat.reshape(3, 1024, 128),
+        y_inverse, x_inverse, x_forward, y_forward, z_forward,
+    ]
     adjoint, grad = pl.pallas_call(
         kernel,
         out_shape=(
             jax.ShapeDtypeStruct((3, 1024, 128), F32),
-            jax.ShapeDtypeStruct((8, 128), F32),
+            jax.ShapeDtypeStruct((1, count), F32),
         ),
-        in_specs=[vmem, smem] + [vmem] * 10,
+        in_specs=[smem, vmem] + [pl.BlockSpec(memory_space=pl.ANY)] * 10,
         out_specs=(vmem, vmem),
-        scratch_shapes=[
+        scratch_shapes=[pltpu.VMEM(each.shape, each.dtype) for each in operands] + [
             pltpu.VMEM((3, 1024, 128), F32),
             pltpu.VMEM((10, RING, RINGS, 8, 128), F32),
             pltpu.VMEM((5, RINGS, 16, NX), F32),
@@ -541,21 +592,18 @@
             pltpu.VMEM((RINGS + 1, 8, 128), F32),
             dma((10,)), dma((10,)), dma((10,)), dma((10,)),
             dma((5,)), dma((5,)), dma((5,)), dma((5,)),
-            dma((1,)), dma((1,)), dma((2,)), dma((2,)),
+            dma((1,)), dma((1,)), dma((2,)), dma((2,)), dma((9,)),
         ],
         compiler_params=pltpu.CompilerParams(
             collective_id=0, has_side_effects=True, vmem_limit_bytes=60 * 1024 * 1024
         ),
     )(
-        velocity_hat.reshape(3, 1024, 128),
         inflow,
+        turbines,
         viscosity,
-        cot_hat.reshape(3, 1024, 128),
-        mode_mask.reshape(512, 128),
-        turbines,
-        *[jnp.asarray(t) for t in tables()],
+        *operands,
     )
-    return adjoint.reshape(velocity_hat.shape), grad[0, :count]
+    return adjoint.reshape(velocity_hat.shape), grad.reshape(count)
 
 
 def solution(mesh):

time: 149 us -> 127 us (0.85)
  Pallas kernels: 142 us -> 119 us
    pallas_call x1, Pallas kernels: 142 us -> 119 us  [local(): pl.pallas_call(kernel, out_shape=(jax.ShapeDtypeStruct((3, 1024, 128), F3...]
    unnamed x1 -> x4, local copies, waits for them, and re-layouts: 2.65 us -> 3.17 us
where the time goes in v3:
time: 127 us; the launch traced here: 126 us
  Pallas kernels  119 us (94%)
  local copies, waits for them, and re-layouts  3.84 us (3%)
  other arithmetic  2.14 us (2%)
    pallas_call x1, Pallas kernels, local(): pl.pallas_call(kernel, out_shape=(jax.ShapeDtypeStruct((3, 1024, 128), F3...  119 us
    unnamed x4, local copies, waits for them, and re-layouts  3.17 us

profile of v3, /device:TPU:0, one launch (start us, length us, event | category | flops | bytes accessed | tf_op | source)
XLA Modules:
  0.0 126.1 jit_solution(10170273053066633080)
XLA Ops:
  0.6 0.7 convert_element_type.21
  1.3 0.7 pad.16
  2.0 0.8 convert_bitcast_fusion.2
  2.8 0.7 select_select_fusion.turb_ref
  3.5 119.4 %shard_map.149 = (f32[3,1024,128]{2,1,0:T(8,128)}, f32[1,100]{1,0:T(1,128)}) custom-call(f32[3]{0:T(128)} %inflow_ref.1, f32[8,128]{1,0:T(8,128)} %select_select_fusion.turb_ref, f32[4,64,512]{2,1,0:T(8,128)} %visc_ref.1, f32[3,1024,128]{2,1,0:T(8,128)} %bitcast.11, s32[512,128]{1,0:T(8,128)} %bitcast.14, bf16[2,256,256]{2,1,0:T(8,128)(2,1)} %constant.26.clone.refs_2_, ...), custom_call_target="tpu_custom_call" | custom-call | tf_op jit(solution)/shard_map/pallas_call | solution.py:570
  122.9 0.0 copy-start
  122.9 2.7 %copy.18 = f32[3,2,64,8,128]{4,3,2,1,0:T(8,128)} copy(f32[3,2,64,8,128]{4,3,2,1,0:T(8,128)} %bitcast.13) | data formatting | bytes 3145728
  125.5 0.0 copy-done
  125.5 0.5 copy.19
  (7 shorter events, 0.0 us)
Async XLA Ops:
  122.9 2.7 %copy-start = (f32[1,100]{1,0:T(1,128)S(1)}, f32[1,100]{1,0:T(1,128)}, u32[]{:S(2)}) copy-start(f32[1,100]{1,0:T(1,128)} %get-tuple-element.5) | copy-start | bytes 1204

commit v4 on v3

--- a/solution.py
+++ b/solution.py
@@ -80,14 +80,14 @@
 
 
 def kernel(
-    inflow_ref, turb_ref, visc_ref, *refs,
+    inflow_ref, hub_ref, sector_ref, thrust_ref, visc_ref, *refs,
 ):
     held, refs = refs[:9], refs[9:]
     (out_ref, grad_ref), refs = refs[:2], refs[2:]
     loaded, refs = refs[:9], refs[9:]
     cot_ref, mask_ref, zi_ref, modes_ref, yi_ref, xi_ref, xf_ref, yf_ref, zf_ref = loaded
     (
-        adj, sent, ring, sheet, plane, phys, visc, rows, fold, turned, pencil, part, part_a, part_b,
+        adj, sent, ring, sheet, plane, phys, visc, rows, fold, turned, pencil, part, part_a, part_b, turbine,
         s1, r1, s2, r2, s3, r3, s4, r4, sv, rv, sa, ra, load,
     ) = refs
     gy = lax.axis_index("gy")
@@ -130,7 +130,6 @@
     loads = [pltpu.make_async_copy(held[k], loaded[k], load.at[k]) for k in range(9)]
     for copy in loads:
         copy.start()
-    pl.semaphore_wait(barrier, RING + RINGS - 2)
 
     def exchange(steps, target, device, source, landing, send, receive):
         @pl.loop(1, steps)
@@ -162,18 +161,6 @@
 
     def octet(index):
         return pl.ds(pl.multiple_of(index * 8, 8), 8)
-
-    landing = visc.at[pl.ds(pl.multiple_of(gy * 64, 64), 64)]
-
-    @pl.loop(1, 4)
-    def _(step):
-        other = (gy + step) % 4
-        pltpu.make_async_remote_copy(
-            src_ref=visc_ref.at[other], dst_ref=landing, send_sem=sv.at[0], recv_sem=rv.at[0],
-            device_id={"gy": other, "gz": gz}, device_id_type=MESH,
-        ).start()
-
-    pltpu.make_async_copy(visc_ref.at[gy], landing, rv.at[0]).start()
 
     def tile_waves(kx):
         wave_x = (2.0 * math.pi / NX) * (gy * WIDTH + kx).astype(F32)
@@ -226,7 +213,11 @@
         to_sheets(lambda k: ring.at[f, k], plane.at[f, w], s2.at[f], r2.at[f])
 
     def pull_first(f):
-        to_sheets(lambda k: sent.at[f, :, k], sheet.at[f - 5, w], s1.at[f], r1.at[f])
+        to_sheets(lambda k: sent.at[f, :, k], sheet.at[f - 4, w], s1.at[f], r1.at[f])
+
+    def last_second():
+        drain(sheet.at[0], r1.at[4])
+        to_rings(lambda k: sheet.at[0, :, k], plane.at[4, :, octet(z_lo), lanes(gy)], s2.at[4], r2.at[4])
 
     def pull_second(f):
         @pl.when(kept_x)
@@ -235,29 +226,57 @@
             for first, count in ((0, 4), (4 + 5 * z_lo, 3), (12, 4)):
                 some = pl.ds(first, count)
                 to_rings(
-                    lambda k: sheet.at[f - 5, some, k], plane.at[f + 1, some, octet(z_lo), lanes(gy)],
+                    lambda k: sheet.at[f - 4, some, k], plane.at[f + 1, some, octet(z_lo), lanes(gy)],
                     s2.at[f], r2.at[f],
                 )
 
+    def send_visc():
+        landing = visc.at[pl.ds(pl.multiple_of(gy * 64, 64), 64)]
+
+        @pl.loop(1, 4)
+        def _(step):
+            other = (gy + step) % 4
+            pltpu.make_async_remote_copy(
+                src_ref=visc_ref.at[other], dst_ref=landing, send_sem=sv.at[0], recv_sem=rv.at[0],
+                device_id={"gy": other, "gz": gz}, device_id_type=MESH,
+            ).start()
+
+        pltpu.make_async_copy(visc_ref.at[gy], landing, rv.at[0]).start()
+
+    def pull_fields(f):
+        pull_first(5 + f)
+
+        @pl.when(f < 2)
+        def _():
+            pull_first(8 + f)
+
     loads[2].wait()
 
-    @pl.loop(0, 3)
+    @pl.when(kept)
+    def _():
+        z_inverse(adj, 0, 5)
+
+    loads[3].wait()
+    z_inverse(modes_ref, 0, 0)
+    pl.semaphore_wait(barrier, RING + RINGS - 2)
+
+    @pl.when(kept)
+    def _():
+        pull_fields(0)
+
+    flow_first(0)
+    @pl.loop(1, 3)
     def _(f):
         @pl.when(kept)
         def _():
             z_inverse(adj, f, 5)
-            pull_first(5 + f)
-
-            @pl.when(f < 2)
-            def _():
-                pull_first(8 + f)
-
-    loads[3].wait()
-
-    @pl.loop(0, 3)
-    def _(f):
+            pull_fields(f)
+
         z_inverse(modes_ref, f, 0)
-        flow_first(f)
+
+        @pl.when(f == 1)
+        def _():
+            flow_first(1)
 
     @pl.loop(6, 11)
     def _(slot):
@@ -266,15 +285,11 @@
         plane[slot, 7:9, :, :384] = jnp.zeros((2, 16, 384), F32)
         plane[slot, 9:12, :8, :384] = jnp.zeros((3, 8, 384), F32)
 
-    @pl.loop(0, 3)
-    def _(f):
-        pull_second(5 + f)
-        flow_second(f)
-
+    pull_second(5)
     pull_second(8)
-    pull_second(9)
-    flow_first(3)
-    flow_first(4)
+    flow_second(0)
+    pull_second(6)
+    flow_first(2)
     for copy in loads[4:]:
         copy.wait()
 
@@ -313,35 +328,12 @@
             done = three(moved, (xi_ref[0, :, cols], xi_ref[1, :, cols]))
             phys[index, :, cols] = done
 
-    @pl.loop(0, 9)
-    def _(task):
-        @pl.when(task < 3)
-        def _():
-            drain_tiles(66, r2.at[5 + task])
-
-        @pl.when(task == 3)
-        def _():
-            drain(plane.at[0], r2.at[0])
-
-        @pl.when(task == 4)
-        def _():
-            drain_tiles(66, r2.at[8])
-            drain_tiles(66, r2.at[9])
-            curl(6, (3, 4, 5))
-
-        @pl.when(task == 7)
-        def _():
-            drain(plane.at[1], r2.at[1])
-
-        @pl.when(task == 8)
-        def _():
-            flow_second(3)
-            drain(plane.at[2], r2.at[2])
-
-        to_cells(jnp.where(task < 3, task + 6, jnp.where(task == 3, 0, jnp.where(task < 7, task + 5, task - 6))))
-
-    hub_x, hub_y, hub_z = turb_ref[0:1, :], turb_ref[1:2, :], turb_ref[2:3, :]
-    sector, thrust = turb_ref[3:4, :], turb_ref[4:5, :]
+    count = thrust_ref.shape[1]
+    turbine[...] = jnp.full((8, 128), -1000.0, F32)
+    turbine[0:3, :count] = hub_ref[...].astype(F32)
+    turbine[3:4, :count] = sector_ref[...].astype(F32)
+    turbine[4:5, :count] = thrust_ref[...]
+    hub_x, hub_y, hub_z, sector, thrust = [turbine[k : k + 1, :] for k in range(5)]
     normal_x = normal_y = jnp.zeros((1, 128), F32)
     for k in range(13):
         angle = (k - 6) * math.pi / 36.0
@@ -361,10 +353,47 @@
         mixed = normal_x * column(first, inflow[0]) + normal_y * column(first + 1, inflow[1])
         return jnp.sum(disk * mixed, axis=0, keepdims=True)
 
-    part[...] = jnp.zeros((8, 128), F32)
-    part[0:1, :] = project(0, (inflow_ref[0], inflow_ref[1]))
-    part[1:2, :] = project(6, (0.0, 0.0))
-    to_rings(lambda k: part, part_a.at[e], sa.at[0], ra.at[0])
+    @pl.loop(0, 9)
+    def _(task):
+        @pl.when(task == 0)
+        def _():
+            drain_tiles(66, r2.at[5])
+
+        @pl.when(task == 1)
+        def _():
+            flow_second(1)
+            pull_second(9)
+            drain_tiles(66, r2.at[6])
+
+        @pl.when(task == 2)
+        def _():
+            pull_second(7)
+            send_visc()
+            flow_first(3)
+            flow_second(2)
+            pull_first(4)
+            drain(plane.at[0], r2.at[0])
+
+        @pl.when(task == 3)
+        def _():
+            for f in (7, 8, 9):
+                drain_tiles(66, r2.at[f])
+            curl(6, (3, 4, 5))
+
+        @pl.when(task == 7)
+        def _():
+            drain(plane.at[1], r2.at[1])
+
+        @pl.when(task == 8)
+        def _():
+            part[...] = jnp.zeros((8, 128), F32)
+            part[0:1, :] = project(0, (inflow_ref[0], inflow_ref[1]))
+            part[1:2, :] = project(6, (0.0, 0.0))
+            to_rings(lambda k: part, part_a.at[e], sa.at[0], ra.at[0])
+            drain(plane.at[2], r2.at[2])
+
+        to_cells(jnp.where(task < 2, task + 6, jnp.where(task == 2, 0, jnp.where(task < 7, task + 5, task - 6))))
+
     drain(visc, rv.at[0])
 
     @pl.loop(0, 32)
@@ -378,12 +407,7 @@
         phys[10, at] = p2 * u0 - p0 * u2 - nu * q1
         phys[11, at] = p0 * u1 - p1 * u0 - nu * q2
 
-    drain(part_a, ra.at[0])
-    total = part_a[0]
-    for k in range(1, RING):
-        total = total + part_a[k]
-    part_b[RINGS] = total
-    to_sheets(lambda k: part_b.at[RINGS], part_b.at[w], sa.at[1], ra.at[1])
+    flow_second(3)
 
     def to_modes(source, target):
         moved = halves(phys[source])
@@ -396,19 +420,19 @@
     def mine(ref, k):
         return ref.at[:, octet(k // 4), lanes(k % 4)]
 
-    def even_first(k, slot):
-        to_sheets(lambda other: plane.at[slot, other], fold.at[k // 2, w], s3.at[k], r3.at[k])
-
-    def even_second(k):
-        drain(fold.at[k // 2], r3.at[k])
-        to_rings(lambda other: mine(fold.at[k // 2], other), pencil.at[k, e], s4.at[k], r4.at[k])
-
-    def odd_first(k, slot):
-        to_rings(lambda other: mine(plane.at[slot], other), turned.at[k // 2, e], s3.at[k], r3.at[k])
-
-    def odd_second(k):
-        drain(turned.at[k // 2], r3.at[k])
-        to_sheets(lambda other: turned.at[k // 2, :, other], pencil.at[k, :, w], s4.at[k], r4.at[k])
+    def sheet_first(k, slot, at):
+        to_sheets(lambda other: plane.at[slot, other], fold.at[at, w], s3.at[k], r3.at[k])
+
+    def sheet_second(k, at):
+        drain(fold.at[at], r3.at[k])
+        to_rings(lambda other: mine(fold.at[at], other), pencil.at[k, e], s4.at[k], r4.at[k])
+
+    def ring_first(k, slot, at):
+        to_rings(lambda other: mine(plane.at[slot], other), turned.at[at, e], s3.at[k], r3.at[k])
+
+    def ring_second(k, at):
+        drain(turned.at[at], r3.at[k])
+        to_sheets(lambda other: turned.at[at, :, other], pencil.at[k, :, w], s4.at[k], r4.at[k])
 
     @pl.loop(0, 3)
     def _(j):
@@ -416,24 +440,21 @@
 
         @pl.when(j == 0)
         def _():
-            even_first(0, 6)
-            flow_second(4)
+            ring_first(0, 6, 0)
+            drain(part_a, ra.at[0])
+            total = part_a[0]
+            for k in range(1, RING):
+                total = total + part_a[k]
+            part_b[RINGS] = total
+            to_sheets(lambda k: part_b.at[RINGS], part_b.at[w], sa.at[1], ra.at[1])
+            last_second()
 
         @pl.when(j == 1)
         def _():
-            odd_first(1, 7)
+            sheet_first(1, 7, 0)
 
     curl(0, (5,))
     to_cells(5)
-    drain(plane.at[3], r2.at[3])
-    curl(0, (3,))
-    to_cells(3)
-
-    @pl.loop(0, 32)
-    def _(block):
-        at = octet(block)
-        phys[9, at] = phys[3, at] * phys[8, at] - phys[5, at] * phys[7, at]
-
     drain(part_b.at[pl.ds(0, RINGS)], ra.at[1])
     total = part_b[0]
     for k in range(1, RINGS):
@@ -444,19 +465,27 @@
     grad_ref[...] = grad[:, : grad_ref.shape[1]]
     weight = -thrust * jnp.abs(disk_speed) * push / disk_area()
 
-    def add_force(index, normal):
+    for index, normal in ((9, normal_x), (10, normal_y)):
         high, low = halves(disk * (weight * normal))
-        phys[index] = phys[index] + dot_nt(high, hot) + dot_nt(low, hot)
-
-    add_force(9, normal_x)
+        phys[index] = dot_nt(high, hot) + dot_nt(low, hot)
+
+    drain(plane.at[3], r2.at[3])
+    curl(0, (3,))
+    to_cells(3)
+
+    @pl.loop(0, 32)
+    def _(block):
+        at = octet(block)
+        phys[9, at] = phys[9, at] + phys[3, at] * phys[8, at] - phys[5, at] * phys[7, at]
+
     to_modes(9, 9)
 
     @pl.loop(0, RINGS)
     def _(block):
         plane[9, block] = plane[9, block] + wave_y_of(block) * turn(plane[8, block])
 
-    even_first(2, 9)
-    odd_second(1)
+    ring_first(2, 9, 1)
+    ring_second(0, 0)
     drain(plane.at[4], r2.at[4])
     curl(0, (4,))
     to_cells(4)
@@ -466,10 +495,8 @@
         at = octet(block)
         w1, w0, w2 = [phys[3 + k, at] for k in range(3)]
         p0, p1, p2 = [phys[6 + k, at] for k in range(3)]
-        phys[10, at] = w2 * p0 - w0 * p2
+        phys[10, at] = phys[10, at] + w2 * p0 - w0 * p2
         phys[11, at] = w0 * p1 - w1 * p0
-
-    add_force(10, normal_y)
 
     @pl.loop(1, 3)
     def _(j):
@@ -489,16 +516,16 @@
 
         @pl.when(j == 1)
         def _():
-            odd_first(3, 10)
-            even_second(0)
+            sheet_first(3, 10, 1)
+            sheet_second(1, 0)
 
         @pl.when(j == 2)
         def _():
-            even_first(4, 11)
-
-    even_second(2)
-    odd_second(3)
-    even_second(4)
+            sheet_first(4, 11, 2)
+
+    ring_second(2, 1)
+    sheet_second(3, 1)
+    sheet_second(4, 2)
     pencils = pencil.reshape(5, 1024, 128)
 
     def z_forward(f, table, fields):
@@ -523,28 +550,24 @@
     drain(pencil.at[4], r4.at[4])
     z_forward(2, (zf_ref[0, 0, :, :256], zf_ref[1, 0, :, :256]), (4,))
 
-    @pl.loop(0, 5)
-    def _(f):
+    for f in range(4):
         drain_tiles(112, s1.at[f])
         drain_tiles(120, s2.at[f])
-
-        @pl.when(kept)
-        def _():
-            drain_tiles(120, s1.at[5 + f])
-
-        @pl.when(kept_x)
-        def _():
-            drain_tiles(77, s2.at[5 + f])
-
-        @pl.when(f % 2 == 0)
-        def _():
-            drain_tiles(120, s3.at[f])
-            drain_tiles(112, s4.at[f])
-
-        @pl.when(f % 2 == 1)
-        def _():
-            drain_tiles(112, s3.at[f])
-            drain_tiles(120, s4.at[f])
+    drain_tiles(120, s1.at[4])
+    drain_tiles(112, s2.at[4])
+    for k in range(5):
+        drain_tiles(112 if k in (0, 2) else 120, s3.at[k])
+        drain_tiles(120 if k in (0, 2) else 112, s4.at[k])
+
+    @pl.when(kept)
+    def _():
+        for f in range(5, 10):
+            drain_tiles(120, s1.at[f])
+
+    @pl.when(kept_x)
+    def _():
+        for f in range(5, 10):
+            drain_tiles(77, s2.at[f])
 
     drain(visc.at[pl.ds(0, 192)], sv.at[0])
     drain(part_a.at[pl.ds(0, RING - 1)], sa.at[0])
@@ -553,12 +576,6 @@
 
 def local(velocity_hat, inflow, viscosity, cot_hat, mode_mask, hub_cells, yaw_sector, thrust):
     count = thrust.shape[0]
-    row = lax.broadcasted_iota(jnp.int32, (8, 128), 0)
-    turbines = jnp.zeros((8, 128), F32)
-    columns = [hub_cells[:, 0], hub_cells[:, 1], hub_cells[:, 2], yaw_sector, thrust]
-    for k, column in enumerate(columns):
-        padded = jnp.pad(column.astype(F32), (0, 128 - count), constant_values=-1000.0)
-        turbines = jnp.where(row == k, padded[None, :], turbines)
     vmem = pl.BlockSpec(memory_space=pltpu.VMEM)
     smem = pl.BlockSpec(memory_space=pltpu.SMEM)
     dma = pltpu.SemaphoreType.DMA
@@ -573,13 +590,13 @@
             jax.ShapeDtypeStruct((3, 1024, 128), F32),
             jax.ShapeDtypeStruct((1, count), F32),
         ),
-        in_specs=[smem, vmem] + [pl.BlockSpec(memory_space=pl.ANY)] * 10,
+        in_specs=[smem, vmem, vmem, vmem] + [pl.BlockSpec(memory_space=pl.ANY)] * 10,
         out_specs=(vmem, vmem),
         scratch_shapes=[pltpu.VMEM(each.shape, each.dtype) for each in operands] + [
             pltpu.VMEM((3, 1024, 128), F32),
             pltpu.VMEM((10, RING, RINGS, 8, 128), F32),
-            pltpu.VMEM((5, RINGS, 16, NX), F32),
-            pltpu.VMEM((5, RINGS, RING, 8, 128), F32),
+            pltpu.VMEM((4, RINGS, 16, NX), F32),
+            pltpu.VMEM((6, RINGS, RING, 8, 128), F32),
             pltpu.VMEM((12, RINGS, 16, NX), F32),
             pltpu.VMEM((12, NY, NX), F32),
             pltpu.VMEM((NY, NX), F32),
@@ -590,6 +607,7 @@
             pltpu.VMEM((8, 128), F32),
             pltpu.VMEM((RING, 8, 128), F32),
             pltpu.VMEM((RINGS + 1, 8, 128), F32),
+            pltpu.VMEM((8, 128), F32),
             dma((10,)), dma((10,)), dma((10,)), dma((10,)),
             dma((5,)), dma((5,)), dma((5,)), dma((5,)),
             dma((1,)), dma((1,)), dma((2,)), dma((2,)), dma((9,)),
@@ -599,7 +617,9 @@
         ),
     )(
         inflow,
-        turbines,
+        hub_cells.T,
+        yaw_sector.reshape(1, count),
+        thrust.reshape(1, count),
         viscosity,
         *operands,
     )

time: 127 us -> 117 us (0.921)
  Pallas kernels: 119 us -> 112 us
  other arithmetic: 2.14 us -> 0 us
    pallas_call x1, Pallas kernels: 119 us -> 112 us  [local(): pl.pallas_call(kernel, out_shape=(jax.ShapeDtypeStruct((3, 1024, 128), F3...]
    convert_element_type x2 -> x0, other arithmetic: 1.46 us -> none  [local(): column.astype(F32)]
where the time goes in v4:
time: 117 us; the launch traced here: 116 us
  Pallas kernels  112 us (96%)
  local copies, waits for them, and re-layouts  3.17 us (3%)
    pallas_call x1, Pallas kernels, local(): pl.pallas_call(kernel, out_shape=(jax.ShapeDtypeStruct((3, 1024, 128), F3...  112 us
    unnamed x4, local copies, waits for them, and re-layouts  3.17 us

profile of v4, /device:TPU:0, one launch (start us, length us, event | category | flops | bytes accessed | tf_op | source)
XLA Modules:
  0.0 116.1 jit_solution(15216731410105926210)
XLA Ops:
  0.6 112.3 %shard_map.149 = (f32[3,1024,128]{2,1,0:T(8,128)}, f32[1,100]{1,0:T(1,128)}) custom-call(f32[3]{0:T(128)} %inflow_ref.1, s32[3,100]{1,0:T(4,128)} %bitcast.12, s32[1,100]{1,0:T(1,128)} %bitcast.13, f32[1,100]{1,0:T(1,128)} %bitcast.14, f32[4,64,512]{2,1,0:T(8,128)} %visc_ref.1, f32[3,1024,128]{2,1,0:T(8,128)} %bitcast.9, s32[512,128]{1,0:T(8,128)} %bitcast.11, ...), custom_call_target="tpu_custom_call" | custom-call | tf_op jit(solution)/shard_map/pallas_call | solution.py:587
  113.0 0.0 copy-start
  113.0 2.7 %copy.18 = f32[3,2,64,8,128]{4,3,2,1,0:T(8,128)} copy(f32[3,2,64,8,128]{4,3,2,1,0:T(8,128)} %bitcast.8) | data formatting | bytes 3145728
  115.6 0.0 copy-done
  115.6 0.5 copy.19
Async XLA Ops:
  113.0 2.7 %copy-start = (f32[1,100]{1,0:T(1,128)S(1)}, f32[1,100]{1,0:T(1,128)}, u32[]{:S(2)}) copy-start(f32[1,100]{1,0:T(1,128)} %get-tuple-element.5) | copy-start | bytes 1204

commit v5 on v4

--- a/solution.py
+++ b/solution.py
@@ -49,17 +49,16 @@
     row = np.arange(NY)
     w, z_lo, r = row // 16, row // 8 % 2, row % 8
     mode_y = (w // 4) * 64 + z_lo * 32 + (w % 4) * 8 + r
-    angle = 2.0 * math.pi / NY * (np.arange(NY)[:, None] * mode_y[None, :] % NY)
+    angle = 2.0 * math.pi / NY * (np.arange(NY // 2 + 1)[:, None] * mode_y[None, :] % NY)
     cos, sin = np.cos(angle), np.sin(angle)
-    y_inverse = np.concatenate([cos, sin])
-    y_forward = np.concatenate([cos.T, sin.T])
+    y_inverse = np.concatenate([cos, sin[1 : NY // 2]])
     lane = np.arange(NX)
     mode_x = lane // 128 * WIDTH + lane % WIDTH
     weight = np.where(mode_x == 0, 1.0, 2.0) / math.sqrt(NX * NY * NZ)
     angle = 2.0 * math.pi / NX * (mode_x[:, None] * np.arange(NX)[None, :] % NX)
     real = (lane % 128 < WIDTH)[:, None]
     x_inverse = weight[:, None] * np.where(real, np.cos(angle), -np.sin(angle))
-    return [split(t) for t in (z_inverse, np.stack([z_first, z_second]), y_inverse, y_forward, x_inverse, x_inverse.T)]
+    return [split(t) for t in (z_inverse, np.stack([z_first, z_second]), y_inverse, y_inverse.T, x_inverse, x_inverse.T)]
 
 
 def halves(value):
@@ -246,9 +245,13 @@
     def pull_fields(f):
         pull_first(5 + f)
 
-        @pl.when(f < 2)
-        def _():
-            pull_first(8 + f)
+        @pl.when(f == 0)
+        def _():
+            pull_first(8)
+
+        @pl.when(f == 2)
+        def _():
+            pull_first(9)
 
     loads[2].wait()
 
@@ -317,11 +320,17 @@
             if 5 in slots:
                 plane[base + 5, block] = wave_x * turn(plane[base + 1, block]) - wave_y * turn(plane[base, block])
 
+    half = NY // 2
+    edge = lax.broadcasted_iota(jnp.int32, (half, 256), 0) == 0
+
     def to_cells(index):
         for h in range(2):
             cols = pl.ds(h * 256, 256)
             both = three((yi_ref[0], yi_ref[1]), halves(plane[index, :, :, cols].reshape(NY, 256)))
-            rows[:, cols] = both[:NY] + turn(both[NY:])
+            top, low = both[:half], both[half:]
+            spun = turn(low)
+            rows[:half, cols] = jnp.where(edge, top, top + spun)
+            rows[half:, cols] = jnp.where(edge, low, top - spun)
         moved = halves(rows[...])
         for h in range(2):
             cols = pl.ds(h * 256, 256)
@@ -341,7 +350,9 @@
         normal_y = jnp.where(sector == float(k), math.sin(angle), normal_y)
     cell_x = lax.broadcasted_iota(jnp.int32, (NX, 128), 0).astype(F32)
     hot = jnp.where(cell_x == hub_x, 1.0, 0.0).astype(BF16)
-    off_y = lax.broadcasted_iota(jnp.int32, (NY, 128), 0).astype(F32) - hub_y
+    cell_y = lax.broadcasted_iota(jnp.int32, (NY, 128), 0)
+    cell_y = jnp.where(cell_y > half, NY + half - cell_y, cell_y)
+    off_y = cell_y.astype(F32) - hub_y
     off_z = (gz * 4 + gy).astype(F32) - hub_z
     disk = jnp.where(off_y * off_y + off_z * off_z <= float(RADIUS * RADIUS), 1.0, 0.0)
 
@@ -362,23 +373,32 @@
         @pl.when(task == 1)
         def _():
             flow_second(1)
+            pull_second(7)
+            drain_tiles(66, r2.at[6])
+
+        @pl.when(task == 2)
+        def _():
+            curl(6, (5,))
+
+        @pl.when(task == 3)
+        def _():
             pull_second(9)
-            drain_tiles(66, r2.at[6])
-
-        @pl.when(task == 2)
-        def _():
-            pull_second(7)
             send_visc()
             flow_first(3)
             flow_second(2)
             pull_first(4)
+            drain_tiles(66, r2.at[7])
+            drain_tiles(66, r2.at[8])
+            curl(6, (3,))
+
+        @pl.when(task == 5)
+        def _():
             drain(plane.at[0], r2.at[0])
 
-        @pl.when(task == 3)
-        def _():
-            for f in (7, 8, 9):
-                drain_tiles(66, r2.at[f])
-            curl(6, (3, 4, 5))
+        @pl.when(task == 6)
+        def _():
+            drain_tiles(66, r2.at[9])
+            curl(6, (4,))
 
         @pl.when(task == 7)
         def _():
@@ -392,9 +412,17 @@
             to_rings(lambda k: part, part_a.at[e], sa.at[0], ra.at[0])
             drain(plane.at[2], r2.at[2])
 
-        to_cells(jnp.where(task < 2, task + 6, jnp.where(task == 2, 0, jnp.where(task < 7, task + 5, task - 6))))
+        slot = jnp.int32(0)
+        for step, value in enumerate((6, 7, 11, 9, 8, 0, 10, 1, 2)):
+            slot = jnp.where(task == step, value, slot)
+        to_cells(slot)
 
     drain(visc, rv.at[0])
+    first = lax.broadcasted_iota(jnp.int32, (half, half), 0)
+    second = lax.broadcasted_iota(jnp.int32, (half, half), 1)
+    swap = jnp.where((first + second) % half == 0, 1.0, 0.0).astype(BF16)
+    high, low = halves(visc[half:])
+    visc[half:] = dot(swap, high) + dot(swap, low)
 
     @pl.loop(0, 32)
     def _(block):
@@ -414,8 +442,11 @@
         for h in range(2):
             cols = pl.ds(h * 256, 256)
             spectrum = three(moved, (xf_ref[0, :, cols], xf_ref[1, :, cols]))
-            both = three((yf_ref[0], yf_ref[1]), halves(spectrum))
-            plane[target, :, :, cols] = (both[:NY] - turn(both[NY:])).reshape(RINGS, 16, 256)
+            top, low = spectrum[:half], spectrum[half:]
+            even = jnp.where(edge, top, top + low)
+            odd = jnp.where(edge, low, turn(low - top))
+            done = three((yf_ref[0], yf_ref[1]), halves(jnp.concatenate([even, odd], 0)))
+            plane[target, :, :, cols] = done.reshape(RINGS, 16, 256)
 
     def mine(ref, k):
         return ref.at[:, octet(k // 4), lanes(k % 4)]
@@ -478,6 +509,7 @@
         at = octet(block)
         phys[9, at] = phys[9, at] + phys[3, at] * phys[8, at] - phys[5, at] * phys[7, at]
 
+    ring_second(0, 0)
     to_modes(9, 9)
 
     @pl.loop(0, RINGS)
@@ -485,7 +517,6 @@
         plane[9, block] = plane[9, block] + wave_y_of(block) * turn(plane[8, block])
 
     ring_first(2, 9, 1)
-    ring_second(0, 0)
     drain(plane.at[4], r2.at[4])
     curl(0, (4,))
     to_cells(4)

time: 117 us -> 114 us (0.974)
  Pallas kernels: 112 us -> 109 us
    pallas_call x1, Pallas kernels: 112 us -> 109 us  [local(): pl.pallas_call(kernel, out_shape=(jax.ShapeDtypeStruct((3, 1024, 128), F3...]
where the time goes in v5:
time: 114 us; the launch traced here: 113 us
  Pallas kernels  109 us (96%)
  local copies, waits for them, and re-layouts  3.17 us (3%)
    pallas_call x1, Pallas kernels, local(): pl.pallas_call(kernel, out_shape=(jax.ShapeDtypeStruct((3, 1024, 128), F3...  109 us
    unnamed x4, local copies, waits for them, and re-layouts  3.17 us

profile of v5, /device:TPU:0, one launch (start us, length us, event | category | flops | bytes accessed | tf_op | source)
XLA Modules:
  0.0 112.8 jit_solution(7548918179543708996)
XLA Ops:
  0.6 109.0 %shard_map.149 = (f32[3,1024,128]{2,1,0:T(8,128)}, f32[1,100]{1,0:T(1,128)}) custom-call(f32[3]{0:T(128)} %inflow_ref.1, s32[3,100]{1,0:T(4,128)} %bitcast.12, s32[1,100]{1,0:T(1,128)} %bitcast.13, f32[1,100]{1,0:T(1,128)} %bitcast.14, f32[4,64,512]{2,1,0:T(8,128)} %visc_ref.1, f32[3,1024,128]{2,1,0:T(8,128)} %bitcast.9, s32[512,128]{1,0:T(8,128)} %bitcast.11, ...), custom_call_target="tpu_custom_call" | custom-call | tf_op jit(solution)/shard_map/pallas_call | solution.py:618
  109.6 0.0 copy-start
  109.6 2.7 %copy.18 = f32[3,2,64,8,128]{4,3,2,1,0:T(8,128)} copy(f32[3,2,64,8,128]{4,3,2,1,0:T(8,128)} %bitcast.8) | data formatting | bytes 3145728
  112.3 0.0 copy-done
  112.3 0.5 copy.19
Async XLA Ops:
  109.6 2.7 %copy-start = (f32[1,100]{1,0:T(1,128)S(1)}, f32[1,100]{1,0:T(1,128)}, u32[]{:S(2)}) copy-start(f32[1,100]{1,0:T(1,128)} %get-tuple-element.5) | copy-start | bytes 1204

commit v6 on v5

--- a/solution.py
+++ b/solution.py
@@ -86,8 +86,8 @@
     loaded, refs = refs[:9], refs[9:]
     cot_ref, mask_ref, zi_ref, modes_ref, yi_ref, xi_ref, xf_ref, yf_ref, zf_ref = loaded
     (
-        adj, sent, ring, sheet, plane, phys, visc, rows, fold, turned, pencil, part, part_a, part_b, turbine,
-        s1, r1, s2, r2, s3, r3, s4, r4, sv, rv, sa, ra, load,
+        adj, sent, ring, sheet, plane, phys, visc, rows, fold, turned, pencil, result, part, part_a, part_b, turbine,
+        s1, r1, s2, r2, s3, r3, s4, r4, sv, rv, sa, ra, load, leave,
     ) = refs
     gy = lax.axis_index("gy")
     gz = lax.axis_index("gz")
@@ -437,7 +437,7 @@
 
     flow_second(3)
 
-    def to_modes(source, target):
+    def to_modes(source, target, extra=None):
         moved = halves(phys[source])
         for h in range(2):
             cols = pl.ds(h * 256, 256)
@@ -446,6 +446,8 @@
             even = jnp.where(edge, top, top + low)
             odd = jnp.where(edge, low, turn(low - top))
             done = three((yf_ref[0], yf_ref[1]), halves(jnp.concatenate([even, odd], 0)))
+            if extra is not None:
+                done = done + extra(cols)
             plane[target, :, :, cols] = done.reshape(RINGS, 16, 256)
 
     def mine(ref, k):
@@ -510,12 +512,15 @@
         phys[9, at] = phys[9, at] + phys[3, at] * phys[8, at] - phys[5, at] * phys[7, at]
 
     ring_second(0, 0)
-    to_modes(9, 9)
-
-    @pl.loop(0, RINGS)
-    def _(block):
-        plane[9, block] = plane[9, block] + wave_y_of(block) * turn(plane[8, block])
-
+    spread_y = jnp.concatenate([wave_y_of(block) for block in range(RINGS)], 0)
+
+    def spun(slot, cols):
+        return turn(plane[slot, :, :, cols].reshape(NY, 256))
+
+    def across(cols):
+        return wave_x[:, cols.start : cols.start + 256]
+
+    to_modes(9, 9, lambda cols: spread_y * spun(8, cols))
     ring_first(2, 9, 1)
     drain(plane.at[4], r2.at[4])
     curl(0, (4,))
@@ -529,31 +534,11 @@
         phys[10, at] = phys[10, at] + w2 * p0 - w0 * p2
         phys[11, at] = w0 * p1 - w1 * p0
 
-    @pl.loop(1, 3)
-    def _(j):
-        to_modes(9 + j, 9 + j)
-
-        @pl.loop(0, RINGS)
-        def _(block):
-            own = plane[9 + j, block]
-
-            @pl.when(j == 1)
-            def _():
-                plane[10, block] = own - wave_x * turn(plane[8, block])
-
-            @pl.when(j == 2)
-            def _():
-                plane[11, block] = own + wave_x * turn(plane[7, block]) - wave_y_of(block) * turn(plane[6, block])
-
-        @pl.when(j == 1)
-        def _():
-            sheet_first(3, 10, 1)
-            sheet_second(1, 0)
-
-        @pl.when(j == 2)
-        def _():
-            sheet_first(4, 11, 2)
-
+    to_modes(10, 10, lambda cols: -across(cols) * spun(8, cols))
+    sheet_first(3, 10, 1)
+    sheet_second(1, 0)
+    to_modes(11, 11, lambda cols: across(cols) * spun(7, cols) - spread_y * spun(6, cols))
+    sheet_first(4, 11, 2)
     ring_second(2, 1)
     sheet_second(3, 1)
     sheet_second(4, 2)
@@ -571,7 +556,9 @@
                 doubled = jnp.where(
                     (lax.broadcasted_iota(jnp.int32, (128, 1), 0) % WIDTH == 0) & (gy == 0), 1.0, 2.0
                 )
-                out_ref[f, at, :] = adj[f, at, :] * doubled + SECTION_STEP * done[:, i * 128 : i * 128 + 128].T
+                result[f, at, :] = adj[f, at, :] * doubled + SECTION_STEP * done[:, i * 128 : i * 128 + 128].T
+
+        pltpu.make_async_copy(result.at[f], out_ref.at[f], leave.at[f]).start()
 
     for k in range(3):
         drain(pencil.at[k], r4.at[k])
@@ -600,9 +587,26 @@
         for f in range(5, 10):
             drain_tiles(77, s2.at[f])
 
+    for f in range(3):
+        pltpu.make_async_copy(result.at[f], out_ref.at[f], leave.at[f]).wait()
     drain(visc.at[pl.ds(0, 192)], sv.at[0])
     drain(part_a.at[pl.ds(0, RING - 1)], sa.at[0])
     drain(part_b.at[pl.ds(0, RINGS - 1)], sa.at[1])
+
+
+def carry(adjoint, grad, adjoint_out, grad_out, rest, small, arrive, leave):
+    pieces = [(adjoint.at[f, pl.ds(k * 512, 512)], rest.at[f, pl.ds(k * 512, 512)], adjoint_out.at[f, pl.ds(k * 512, 512)])
+              for f in range(3) for k in range(2)]
+    pieces.append((grad, small, grad_out))
+    inward = [pltpu.make_async_copy(piece[0], piece[1], arrive.at[k]) for k, piece in enumerate(pieces)]
+    outward = [pltpu.make_async_copy(piece[1], piece[2], leave.at[k]) for k, piece in enumerate(pieces)]
+    for copy in inward:
+        copy.start()
+    for first, then in zip(inward, outward):
+        first.wait()
+        then.start()
+    for copy in outward:
+        copy.wait()
 
 
 def local(velocity_hat, inflow, viscosity, cot_hat, mode_mask, hub_cells, yaw_sector, thrust):
@@ -622,7 +626,7 @@
             jax.ShapeDtypeStruct((1, count), F32),
         ),
         in_specs=[smem, vmem, vmem, vmem] + [pl.BlockSpec(memory_space=pl.ANY)] * 10,
-        out_specs=(vmem, vmem),
+        out_specs=(pl.BlockSpec(memory_space=pl.ANY), vmem),
         scratch_shapes=[pltpu.VMEM(each.shape, each.dtype) for each in operands] + [
             pltpu.VMEM((3, 1024, 128), F32),
             pltpu.VMEM((10, RING, RINGS, 8, 128), F32),
@@ -635,13 +639,14 @@
             pltpu.VMEM((3, RINGS, 16, NX), F32),
             pltpu.VMEM((2, RING, RINGS, 8, 128), F32),
             pltpu.VMEM((5, RING, RINGS, 8, 128), F32),
+            pltpu.VMEM((3, 1024, 128), F32),
             pltpu.VMEM((8, 128), F32),
             pltpu.VMEM((RING, 8, 128), F32),
             pltpu.VMEM((RINGS + 1, 8, 128), F32),
             pltpu.VMEM((8, 128), F32),
             dma((10,)), dma((10,)), dma((10,)), dma((10,)),
             dma((5,)), dma((5,)), dma((5,)), dma((5,)),
-            dma((1,)), dma((1,)), dma((2,)), dma((2,)), dma((9,)),
+            dma((1,)), dma((1,)), dma((2,)), dma((2,)), dma((9,)), dma((3,)),
         ],
         compiler_params=pltpu.CompilerParams(
             collective_id=0, has_side_effects=True, vmem_limit_bytes=60 * 1024 * 1024
@@ -654,6 +659,14 @@
         viscosity,
         *operands,
     )
+    whole = pl.BlockSpec(memory_space=pl.ANY)
+    adjoint, grad = pl.pallas_call(
+        carry,
+        out_shape=tuple(jax.ShapeDtypeStruct(each.shape, F32) for each in (adjoint, grad)),
+        in_specs=[whole, whole],
+        out_specs=(whole, whole),
+        scratch_shapes=[pltpu.VMEM(adjoint.shape, F32), pltpu.VMEM(grad.shape, F32), dma((7,)), dma((7,))],
+    )(adjoint, grad)
     return adjoint.reshape(velocity_hat.shape), grad.reshape(count)
 
 

time: 114 us -> 111 us (0.974)
  local copies, waits for them, and re-layouts: 3.17 us -> 0 us
    unnamed x4 -> x0, local copies, waits for them, and re-layouts: 3.17 us -> none
    pallas_call x1, Pallas kernels: 109 us -> 107 us  [local(): pl.pallas_call(kernel, out_shape=(jax.ShapeDtypeStruct((3, 1024, 128), F3...]
    pallas_call x0 -> x1, Pallas kernels: none -> 2.21 us  [local(): pl.pallas_call(carry, out_shape=tuple((jax.ShapeDtypeStruct(each.shape, F...]
where the time goes in v6:
time: 111 us; the launch traced here: 110 us
  Pallas kernels  109 us (98%)
    pallas_call x1, Pallas kernels, local(): pl.pallas_call(kernel, out_shape=(jax.ShapeDtypeStruct((3, 1024, 128), F3...  107 us

profile of v6, /device:TPU:0, one launch (start us, length us, event | category | flops | bytes accessed | tf_op | source)
XLA Modules:
  0.0 109.6 jit_solution(5282288837268049284)
XLA Ops:
  0.6 106.6 %shard_map.149 = (f32[3,1024,128]{2,1,0:T(8,128)}, f32[1,100]{1,0:T(1,128)}) custom-call(f32[3]{0:T(128)} %inflow_ref.1, s32[3,100]{1,0:T(4,128)} %bitcast.11, s32[1,100]{1,0:T(1,128)} %bitcast.12, f32[1,100]{1,0:T(1,128)} %bitcast.13, f32[4,64,512]{2,1,0:T(8,128)} %visc_ref.1, f32[3,1024,128]{2,1,0:T(8,128)} %bitcast.8, s32[512,128]{1,0:T(8,128)} %bitcast.10, ...), custom_call_target="tpu_custom_call" | custom-call | tf_op jit(solution)/shard_map/pallas_call | solution.py:622
  107.2 2.2 %shard_map.150 = (f32[3,1024,128]{2,1,0:T(8,128)}, f32[1,100]{1,0:T(1,128)}) custom-call(f32[3,1024,128]{2,1,0:T(8,128)} %get-tuple-element.6.adjoint, f32[1,100]{1,0:T(1,128)} %get-tuple-element.7.grad), custom_call_target="tpu_custom_call" | custom-call | tf_op jit(solution)/shard_map/pallas_call | solution.py:663

commit v7 on v6

--- a/solution.py
+++ b/solution.py
@@ -387,6 +387,8 @@
             flow_first(3)
             flow_second(2)
             pull_first(4)
+            part[...] = jnp.zeros((8, 128), F32)
+            part[1:2, :] = project(6, (0.0, 0.0))
             drain_tiles(66, r2.at[7])
             drain_tiles(66, r2.at[8])
             curl(6, (3,))
@@ -406,9 +408,7 @@
 
         @pl.when(task == 8)
         def _():
-            part[...] = jnp.zeros((8, 128), F32)
             part[0:1, :] = project(0, (inflow_ref[0], inflow_ref[1]))
-            part[1:2, :] = project(6, (0.0, 0.0))
             to_rings(lambda k: part, part_a.at[e], sa.at[0], ra.at[0])
             drain(plane.at[2], r2.at[2])
 
@@ -417,6 +417,7 @@
             slot = jnp.where(task == step, value, slot)
         to_cells(slot)
 
+    flow_second(3)
     drain(visc, rv.at[0])
     first = lax.broadcasted_iota(jnp.int32, (half, half), 0)
     second = lax.broadcasted_iota(jnp.int32, (half, half), 1)
@@ -434,8 +435,6 @@
         phys[9, at] = p1 * u2 - p2 * u1 - nu * q0
         phys[10, at] = p2 * u0 - p0 * u2 - nu * q1
         phys[11, at] = p0 * u1 - p1 * u0 - nu * q2
-
-    flow_second(3)
 
     def to_modes(source, target, extra=None):
         moved = halves(phys[source])

time: 111 us -> 110 us (level)
  no operation moved by 1% of the time
where the time goes in v7:
time: 110 us; the launch traced here: 109 us
  Pallas kernels  108 us (98%)
    pallas_call x1, Pallas kernels, local(): pl.pallas_call(kernel, out_shape=(jax.ShapeDtypeStruct((3, 1024, 128), F3...  106 us
    pallas_call x1, Pallas kernels, local(): pl.pallas_call(carry, out_shape=tuple((jax.ShapeDtypeStruct(each.shape, F...  2.21 us

profile of v7, /device:TPU:0, one launch (start us, length us, event | category | flops | bytes accessed | tf_op | source)
XLA Modules:
  0.0 109.2 jit_solution(12664544299984236568)
XLA Ops:
  0.6 106.2 %shard_map.149 = (f32[3,1024,128]{2,1,0:T(8,128)}, f32[1,100]{1,0:T(1,128)}) custom-call(f32[3]{0:T(128)} %inflow_ref.1, s32[3,100]{1,0:T(4,128)} %bitcast.11, s32[1,100]{1,0:T(1,128)} %bitcast.12, f32[1,100]{1,0:T(1,128)} %bitcast.13, f32[4,64,512]{2,1,0:T(8,128)} %visc_ref.1, f32[3,1024,128]{2,1,0:T(8,128)} %bitcast.8, s32[512,128]{1,0:T(8,128)} %bitcast.10, ...), custom_call_target="tpu_custom_call" | custom-call | tf_op jit(solution)/shard_map/pallas_call | solution.py:621
  106.9 2.2 %shard_map.150 = (f32[3,1024,128]{2,1,0:T(8,128)}, f32[1,100]{1,0:T(1,128)}) custom-call(f32[3,1024,128]{2,1,0:T(8,128)} %get-tuple-element.6.adjoint, f32[1,100]{1,0:T(1,128)} %get-tuple-element.7.grad), custom_call_target="tpu_custom_call" | custom-call | tf_op jit(solution)/shard_map/pallas_call | solution.py:662
